TPU v7x, 512 devices: a whole 4x8x8 slice. The times are simulated.
512 devices in a mesh: rows: 16 (over y_hi, x), cols: 32 (over y_lo, z, core).
Axes of the slice: x: 4, y: 8 (y_hi: 4, y_lo: 2; y = y_hi * 2 + y_lo), z: 8, core: 2. Of those that a mesh axis runs over, the one named last changes fastest.
Arguments:
- frames: bfloat16 [2, 64, 32768], P(None, 'rows', 'cols'), may hold values from -6 to 6
- hidden_start: bfloat16 [64, 1024, 128], P('rows', 'cols'), may hold values from -3 to 3
- cell_start: float32 [64, 1024, 128], P('rows', 'cols'), may hold values from -6 to 6
- kernel: bfloat16 [1440, 512], replicated, may hold values from -0.15625 to 0.15625
- gate_bias: float32 [512], replicated, may hold values from -4 to 4
- cotangent: bfloat16 [2, 64, 1024, 128], P(None, 'rows', 'cols'), may hold values from -6 to 6
Outputs:
- hidden_final: bfloat16 [64, 1024, 128], P('rows', 'cols')
- grad_hidden_start: float32 [64, 1024, 128], P('rows', 'cols')
- grad_cell_start: float32 [64, 1024, 128], P('rows', 'cols')
- kernel_grad: float32 [1440, 512], replicated
- bias_grad: float32 [512], replicated
All inputs are finite; a program needn't handle non-finite values.
Results may differ from a plain program's by a relative error of at most 0.015.
Values may be sent and summed in bfloat16 or wider, within the bound.
A program may use at most 64 MiB of HBM per device.

v0:
```python
import math

import jax
import jax.numpy as jnp
from jax import lax
from jax.sharding import PartitionSpec as P

HC = 128
CI = 32
KS = 3
STEPS = 2
GATES = 512
KIN = 1440


def extended(cells, sides, width):
    for axis, dim in sides:
        count = lax.axis_size(axis)
        ends = count - 1
        head = lax.slice_in_dim(cells, 0, width, axis=dim)
        tail = lax.slice_in_dim(cells, cells.shape[dim] - width, cells.shape[dim], axis=dim)
        cells = jnp.concatenate(
            [
                lax.ppermute(tail, axis, [(i, (i + 1) % count) for i in range(ends)]),
                cells,
                lax.ppermute(head, axis, [((i + 1) % count, i) for i in range(ends)]),
            ],
            axis=dim,
        )
    return cells


def tap_columns(padded, rows_dev, cols_dev, reverse):
    pieces = []
    for tap_row in range(KS):
        for tap_col in range(KS):
            if reverse:
                first_row = KS - 1 - tap_row
                first_col = KS - 1 - tap_col
            else:
                first_row = tap_row
                first_col = tap_col
            pieces.append(
                padded[first_row : first_row + rows_dev, first_col : first_col + cols_dev]
            )
    joined = jnp.concatenate(pieces, axis=-1)
    return joined.reshape(rows_dev * cols_dev, joined.shape[-1])


def shards(frames, hidden_start, cell_start, kernel, gate_bias, cotangent):
    rows_dev = hidden_start.shape[0]
    cols_dev = hidden_start.shape[1]
    chans = CI + HC
    taps = KS * KS
    cells = rows_dev * cols_dev
    hidden = hidden_start
    cell = cell_start
    saved = []
    for moment in range(STEPS):
        inputs = frames[moment].reshape(rows_dev, cols_dev, CI)
        stacked = jnp.concatenate([inputs, hidden], axis=-1)
        padded = extended(stacked, (("rows", 0), ("cols", 1)), 1)
        patches = tap_columns(padded, rows_dev, cols_dev, False)
        gates = jnp.dot(patches, kernel, preferred_element_type=jnp.float32) + gate_bias
        gates = gates.reshape(rows_dev, cols_dev, GATES)
        gate_in = jax.nn.sigmoid(gates[..., :HC])
        gate_forget = jax.nn.sigmoid(gates[..., HC : 2 * HC])
        gate_cand = jnp.tanh(gates[..., 2 * HC : 3 * HC])
        gate_out = jax.nn.sigmoid(gates[..., 3 * HC :])
        cell_prev = cell
        cell = gate_forget * cell_prev + gate_in * gate_cand
        hidden = (gate_out * jnp.tanh(cell)).astype(jnp.bfloat16)
        saved.append((patches, gate_in, gate_forget, gate_cand, gate_out, cell_prev, cell))
    blocks = kernel.reshape(taps, chans, GATES)
    adjoint_matrix = jnp.transpose(blocks, (0, 2, 1)).reshape(taps * GATES, chans)
    grad_hidden = cotangent[STEPS - 1].astype(jnp.float32)
    grad_cell = jnp.zeros((rows_dev, cols_dev, HC), jnp.float32)
    kernel_acc = jnp.zeros((KIN, GATES), jnp.float32)
    bias_acc = jnp.zeros((GATES,), jnp.float32)
    for moment in range(STEPS - 1, -1, -1):
        patches, gate_in, gate_forget, gate_cand, gate_out, cell_prev, cell_now = saved[moment]
        tanh_cell = jnp.tanh(cell_now)
        summed = grad_cell + grad_hidden * gate_out * (1.0 - tanh_cell * tanh_cell)
        pre_in = summed * gate_cand * gate_in * (1.0 - gate_in)
        pre_forget = summed * cell_prev * gate_forget * (1.0 - gate_forget)
        pre_cand = summed * gate_in * (1.0 - gate_cand * gate_cand)
        pre_out = grad_hidden * tanh_cell * gate_out * (1.0 - gate_out)
        grad_cell = summed * gate_forget
        grad_gates = jnp.concatenate([pre_in, pre_forget, pre_cand, pre_out], axis=-1).astype(
            jnp.bfloat16
        )
        flat_grads = grad_gates.reshape(cells, GATES)
        kernel_acc = kernel_acc + jnp.dot(patches.T, flat_grads, preferred_element_type=jnp.float32)
        bias_acc = bias_acc + jnp.sum(flat_grads.astype(jnp.float32), axis=0)
        grad_padded = extended(grad_gates, (("rows", 0), ("cols", 1)), 1)
        reversed_cols = tap_columns(grad_padded, rows_dev, cols_dev, True)
        grad_stacked = jnp.dot(reversed_cols, adjoint_matrix, preferred_element_type=jnp.float32)
        grad_stacked = grad_stacked.reshape(rows_dev, cols_dev, chans)
        grad_hidden = grad_stacked[..., CI:]
        if moment > 0:
            grad_hidden = grad_hidden + cotangent[moment - 1].astype(jnp.float32)
    kernel_total, bias_total = lax.psum((kernel_acc, bias_acc), ("rows", "cols"))
    total_cells = STEPS * rows_dev * lax.axis_size("rows") * cols_dev * lax.axis_size("cols")
    norm_scale = 1.0 / math.sqrt(total_cells)
    return (hidden, grad_hidden, grad_cell, kernel_total * norm_scale, bias_total * norm_scale)


def solution(mesh):
    placed = (
        P(None, "rows", "cols"),
        P("rows", "cols", None),
        P("rows", "cols", None),
        P(),
        P(),
        P(None, "rows", "cols", None),
    )
    return jax.shard_map(
        shards,
        mesh=mesh,
        in_specs=placed,
        out_specs=(
            P("rows", "cols", None),
            P("rows", "cols", None),
            P("rows", "cols", None),
            P(),
            P(),
        ),
        check_vma=False,
    )
```

profile of v0, /device:TPU:1, one launch (start us, length us, event | category | flops | bytes accessed | tf_op | source)
XLA Modules:
  0.0 496.3 jit_solution(3834109655549823346)
XLA Ops:
  7.2 0.0 all-reduce.2.cloned.1.call-start
  7.2 0.7 fusion.52
  7.9 0.1 reshape_squeeze.7
  8.0 0.8 pad_maximum_fusion.35
  8.8 3.9 collective-permute-start
  12.8 1.3 collective-permute-start.1
  14.1 0.1 concatenate.189
  14.2 0.1 reshape_squeeze.6
  14.3 3.0 collective-permute-done.1
  17.3 0.8 pad_maximum_fusion.52
  18.1 7.3 %collective-permute-start.3 = (bf16[6,1,160]{2,1,0:T(2,128)(2,1)S(1)}, bf16[6,1,160]{2,1,0:T(2,128)(2,1)S(1)}, u32[]{:S(2)}, u32[]{:S(2)}) collective-permute-start(bf16[6,1,160]{2,1,0:T(2,128)(2,1)S(1)} %get-tuple-element.52), channel_id=1, source_target_pairs={{1,0},{2,1},{3,2},{4,3},{5,4},{6,5},{7,6},{8,7},{9,8},{10,9},{11,1... | collective-permute-start | bytes 5768 | tf_op jit(solution)/shard_map/ppermute | solution.py:26
  25.4 2.1 collective-permute-start.2
  27.5 0.9 pad_maximum_fusion.24
  28.4 0.2 collective-permute-done.2
  28.6 0.9 pad_maximum_fusion.18
  29.6 0.3 concatenate.196
  29.9 0.4 convolution_add_fusion.1
  30.3 0.5 copy-done.12
  30.7 0.1 multiply_convert_fusion.8
  30.8 0.1 pad_maximum_fusion.33
  30.9 1.6 collective-permute-start.4
  32.5 1.3 collective-permute-start.5
  33.8 0.1 concatenate.206
  33.9 3.1 collective-permute-done.5
  37.0 0.1 pad_maximum_fusion.48
  37.1 3.4 collective-permute-start.7
  40.5 4.0 collective-permute-start.6
  44.5 0.1 pad_maximum_fusion.20
  44.6 0.6 collective-permute-done.6
  45.2 0.1 pad_maximum_fusion.19
  45.4 0.6 copy-done.4
  46.0 0.0 copy-done.10
  46.1 0.3 concatenate.213
  46.3 0.4 convolution_add_fusion
  46.7 0.5 copy-done.14
  47.2 0.1 multiply_convert_fusion.6
  47.3 0.7 multiply_convert_fusion.5
  48.0 6.3 %collective-permute-start.8 = (bf16[1,32,512]{2,1,0:T(8,128)(2,1)S(1)}, bf16[1,32,512]{2,1,0:T(8,128)(2,1)S(1)}, u32[]{:S(2)}, u32[]{:S(2)}) collective-permute-start(bf16[1,32,512]{2,1,0:T(8,128)(2,1)S(1)} %get-tuple-element.32), channel_id=1, source_target_pairs={{0,32},{32,64},{64,96},{96,128},{128,160},{160,192},{192,224},{224... | collective-permute-start | bytes 98312 | tf_op jit(solution)/shard_map/ppermute | solution.py:24
  54.3 1.3 collective-permute-start.9
  55.6 2.5 copy.14
  58.1 4.0 reshape.83
  62.1 0.3 concatenate.229
  62.4 4.5 collective-permute-start.11
  66.9 1.9 collective-permute-start.10
  68.9 0.3 concatenate.228
  69.1 2.7 collective-permute-done.10
  71.9 0.1 maximum_maximum_fusion
  72.3 1.0 copy-done.1
  73.3 1.1 fusion.46
  74.5 0.1 multiply_convert_fusion.3
  74.6 4.3 collective-permute-start.12
  78.8 1.3 collective-permute-start.13
  80.1 0.6 convolution_bitcast_fusion
  80.7 2.2 fusion
  82.9 119.6 %psum.15 = f32[512]{0:T(512)S(1)} all-reduce(f32[512]{0:T(512)S(1)} %add.68), channel_id=1, replica_groups=mesh['rows'=16,'cols'=32] {'rows','cols'}, use_global_device_ids=true, to_apply=%region_3.0 | all-reduce | flops 512 | bytes 4096 | tf_op jit(solution)/shard_map/psum | solution.py:102
  202.5 3.9 collective-permute-start.15
  206.4 1.9 collective-permute-start.14
  208.4 0.6 broadcast_multiply_fusion.1
  209.0 2.5 collective-permute-done.14
  211.5 0.1 maximum_maximum_fusion.1
  211.9 1.1 copy-done.2
  212.9 1.1 fusion.1
  214.0 271.6 %all-reduce.2.cloned.1.call-done = f32[1440,512]{1,0:T(8,128)} async-done(((f32[1440,512]{1,0:T(8,128)}), f32[1440,512]{1,0:T(8,128)}) %all-reduce.2.cloned.1.call-update) | async-done | bytes 2949136 | tf_op jit(solution)/shard_map/psum | solution.py:102
  485.7 3.8 broadcast_multiply_fusion
  (73 shorter events, 0.8 us)
Async XLA Ops:
  7.2 22.4 %copy-start.3 = (bf16[4,32,128]{2,1,0:T(8,128)(2,1)S(1)}, bf16[4,32,128]{2,1,0:T(8,128)(2,1)}, u32[]{:S(2)}) copy-start(bf16[4,32,128]{2,1,0:T(8,128)(2,1)} %param.7) | copy-start | bytes 98308
  7.2 478.5 %all-reduce.2.cloned.1.call-start = ((), (), s32[]{:S(2)}) async-start(), calls=%async_computation | async-start | bytes 5898240 | tf_op jit(solution)/shard_map/psum | solution.py:102
  8.8 5.4 %collective-permute-start = (bf16[1,32,160]{2,1,0:T(8,128)(2,1)S(1)}, bf16[1,32,160]{2,1,0:T(8,128)(2,1)S(1)}, u32[]{:S(2)}, u32[]{:S(2)}) collective-permute-start(bf16[1,32,160]{2,1,0:T(8,128)(2,1)S(1)} %get-tuple-element.60), channel_id=1, source_target_pairs={{0,32},{32,64},{64,96},{96,128},{128,160},{160,192},{192,224},{224... | collective-permute-start | bytes 30728 | tf_op jit(solution)/shard_map/ppermute | solution.py:24
  12.8 4.5 collective-permute-start.1
  18.1 10.3 %collective-permute-start.3 = (bf16[6,1,160]{2,1,0:T(2,128)(2,1)S(1)}, bf16[6,1,160]{2,1,0:T(2,128)(2,1)S(1)}, u32[]{:S(2)}, u32[]{:S(2)}) collective-permute-start(bf16[6,1,160]{2,1,0:T(2,128)(2,1)S(1)} %get-tuple-element.52), channel_id=1, source_target_pairs={{1,0},{2,1},{3,2},{4,3},{5,4},{6,5},{7,6},{8,7},{9,8},{10,9},{11,1... | collective-permute-start | bytes 5768 | tf_op jit(solution)/shard_map/ppermute | solution.py:26
  25.4 4.5 copy-start
  25.4 4.5 copy-start.16
  25.4 3.2 collective-permute-start.2
  29.9 0.8 copy-start.12
  30.9 3.0 collective-permute-start.4
  32.5 4.5 collective-permute-start.5
  37.1 7.5 %collective-permute-start.7 = (bf16[6,1,160]{2,1,0:T(2,128)(2,1)S(1)}, bf16[6,1,160]{2,1,0:T(2,128)(2,1)S(1)}, u32[]{:S(2)}, u32[]{:S(2)}) collective-permute-start(bf16[6,1,160]{2,1,0:T(2,128)(2,1)S(1)} %get-tuple-element.48), channel_id=1, source_target_pairs={{1,0},{2,1},{3,2},{4,3},{5,4},{6,5},{7,6},{8,7},{9,8},{10,9},{11,1... | collective-permute-start | bytes 5768 | tf_op jit(solution)/shard_map/ppermute | solution.py:26
  40.5 4.7 collective-permute-start.6
  45.4 0.6 copy-start.4
  45.4 0.6 copy-start.6
  45.4 0.6 copy-start.8
  45.4 0.7 copy-start.10
  46.3 0.8 copy-start.14
  48.0 14.3 %collective-permute-start.8 = (bf16[1,32,512]{2,1,0:T(8,128)(2,1)S(1)}, bf16[1,32,512]{2,1,0:T(8,128)(2,1)S(1)}, u32[]{:S(2)}, u32[]{:S(2)}) collective-permute-start(bf16[1,32,512]{2,1,0:T(8,128)(2,1)S(1)} %get-tuple-element.32), channel_id=1, source_target_pairs={{0,32},{32,64},{64,96},{96,128},{128,160},{160,192},{192,224},{224... | collective-permute-start | bytes 98312 | tf_op jit(solution)/shard_map/ppermute | solution.py:24
  54.3 8.0 %collective-permute-start.9 = (bf16[1,32,512]{2,1,0:T(8,128)(2,1)S(1)}, bf16[1,32,512]{2,1,0:T(8,128)(2,1)S(1)}, u32[]{:S(2)}, u32[]{:S(2)}) collective-permute-start(bf16[1,32,512]{2,1,0:T(8,128)(2,1)S(1)} %get-tuple-element.33), channel_id=1, source_target_pairs={{32,0},{64,32},{96,64},{128,96},{160,128},{192,160},{224,192},{256... | collective-permute-start | bytes 98312 | tf_op jit(solution)/shard_map/ppermute | solution.py:26
  62.0 6.8 %copy-start.5 = (bf16[4,32,160]{2,1,0:T(8,128)(2,1)S(1)}, bf16[4,32,160]{2,1,0:T(8,128)(2,1)}, u32[]{:S(2)}) copy-start(bf16[4,32,160]{2,1,0:T(8,128)(2,1)} %copy-done.4) | copy-start | bytes 122884
  62.0 6.8 %copy-start.7 = (bf16[4,32,160]{2,1,0:T(8,128)(2,1)S(1)}, bf16[4,32,160]{2,1,0:T(8,128)(2,1)}, u32[]{:S(2)}) copy-start(bf16[4,32,160]{2,1,0:T(8,128)(2,1)} %copy-done.6) | copy-start | bytes 122884
  62.0 6.8 %copy-start.9 = (bf16[4,32,160]{2,1,0:T(8,128)(2,1)S(1)}, bf16[4,32,160]{2,1,0:T(8,128)(2,1)}, u32[]{:S(2)}) copy-start(bf16[4,32,160]{2,1,0:T(8,128)(2,1)} %copy-done.8) | copy-start | bytes 122884
  62.0 6.8 %copy-start.11 = (bf16[4,32,160]{2,1,0:T(8,128)(2,1)S(1)}, bf16[4,32,160]{2,1,0:T(8,128)(2,1)}, u32[]{:S(2)}) copy-start(bf16[4,32,160]{2,1,0:T(8,128)(2,1)} %copy-done.10) | copy-start | bytes 122884
  62.4 6.8 %collective-permute-start.11 = (bf16[6,1,512]{2,1,0:T(2,128)(2,1)S(1)}, bf16[6,1,512]{2,1,0:T(2,128)(2,1)S(1)}, u32[]{:S(2)}, u32[]{:S(2)}) collective-permute-start(bf16[6,1,512]{2,1,0:T(2,128)(2,1)S(1)} %get-tuple-element.28), channel_id=1, source_target_pairs={{0,1},{1,2},{2,3},{3,4},{4,5},{5,6},{6,7},{7,8},{8,9},{9,10},{10,1... | collective-permute-start | bytes 18440 | tf_op jit(solution)/shard_map/ppermute | solution.py:24
  66.9 5.0 %collective-permute-start.10 = (bf16[6,1,512]{2,1,0:T(2,128)(2,1)S(1)}, bf16[6,1,512]{2,1,0:T(2,128)(2,1)S(1)}, u32[]{:S(2)}, u32[]{:S(2)}) collective-permute-start(bf16[6,1,512]{2,1,0:T(2,128)(2,1)S(1)} %get-tuple-element.29), channel_id=1, source_target_pairs={{1,0},{2,1},{3,2},{4,3},{5,4},{6,5},{7,6},{8,7},{9,8},{10,9},{11,1... | collective-permute-start | bytes 18440 | tf_op jit(solution)/shard_map/ppermute | solution.py:26
  72.0 1.4 copy-start.1
  72.0 1.4 copy-start.15
  73.3 1.1 copy-start.13
  74.6 127.9 %collective-permute-start.12 = (bf16[1,32,512]{2,1,0:T(8,128)(2,1)S(1)}, bf16[1,32,512]{2,1,0:T(8,128)(2,1)S(1)}, u32[]{:S(2)}, u32[]{:S(2)}) collective-permute-start(bf16[1,32,512]{2,1,0:T(8,128)(2,1)S(1)} %get-tuple-element.30), channel_id=1, source_target_pairs={{0,32},{32,64},{64,96},{96,128},{128,160},{160,192},{192,224},{224... | collective-permute-start | bytes 98312 | tf_op jit(solution)/shard_map/ppermute | solution.py:24
  78.8 123.7 %collective-permute-start.13 = (bf16[1,32,512]{2,1,0:T(8,128)(2,1)S(1)}, bf16[1,32,512]{2,1,0:T(8,128)(2,1)S(1)}, u32[]{:S(2)}, u32[]{:S(2)}) collective-permute-start(bf16[1,32,512]{2,1,0:T(8,128)(2,1)S(1)} %get-tuple-element.31), channel_id=1, source_target_pairs={{32,0},{64,32},{96,64},{128,96},{160,128},{192,160},{224,192},{256... | collective-permute-start | bytes 98312 | tf_op jit(solution)/shard_map/ppermute | solution.py:26
  202.5 6.4 %collective-permute-start.15 = (bf16[6,1,512]{2,1,0:T(2,128)(2,1)S(1)}, bf16[6,1,512]{2,1,0:T(2,128)(2,1)S(1)}, u32[]{:S(2)}, u32[]{:S(2)}) collective-permute-start(bf16[6,1,512]{2,1,0:T(2,128)(2,1)S(1)} %get-tuple-element.24), channel_id=1, source_target_pairs={{0,1},{1,2},{2,3},{3,4},{4,5},{5,6},{6,7},{7,8},{8,9},{9,10},{10,1... | collective-permute-start | bytes 18440 | tf_op jit(solution)/shard_map/ppermute | solution.py:24
  206.4 5.0 %collective-permute-start.14 = (bf16[6,1,512]{2,1,0:T(2,128)(2,1)S(1)}, bf16[6,1,512]{2,1,0:T(2,128)(2,1)S(1)}, u32[]{:S(2)}, u32[]{:S(2)}) collective-permute-start(bf16[6,1,512]{2,1,0:T(2,128)(2,1)S(1)} %get-tuple-element.25), channel_id=1, source_target_pairs={{1,0},{2,1},{3,2},{4,3},{5,4},{6,5},{7,6},{8,7},{9,8},{10,9},{11,1... | collective-permute-start | bytes 18440 | tf_op jit(solution)/shard_map/ppermute | solution.py:26
  211.6 1.4 copy-start.2
Sparse Core Ops, SparseCore 0:
  209.1 276.5 all-reduce.1
where the time goes:
time: 498 us; the launch traced here: 496 us
  waiting for transfers between devices  284 us (57%)
  blocking collectives  120 us (24%)
  starting transfers between devices  50.3 us (10%)
  between operations  14.7 us (3%)
  local copies, waits for them, and re-layouts  12.7 us (3%)
  other arithmetic  9.55 us (2%)
  matrix products  5.7 us (1%)
    psum x1, waiting for transfers between devices, shards(): lax.psum((kernel_acc, bias_acc), ('rows', 'cols'))  272 us
    psum x1, blocking collectives, shards(): lax.psum((kernel_acc, bias_acc), ('rows', 'cols'))  120 us
    ppermute x8, starting transfers between devices, extended(): lax.ppermute(tail, axis, [(i, (i + 1) % count) for i in range(ends)])  30.6 us
    ppermute x8, starting transfers between devices, extended(): lax.ppermute(head, axis, [((i + 1) % count, i) for i in range(ends)])  19.6 us
    ppermute x8, waiting for transfers between devices, extended(): lax.ppermute(head, axis, [((i + 1) % count, i) for i in range(ends)])  11.3 us
  transfers between devices with their start and end apart: 17, of which 7 were waited for; matrix products, arithmetic and copies ran while one was open for 3% of the time, Pallas kernels for 0%

commit v1 on v0

v1 whole, which is shorter than its diff:
```python
import functools
import math

import jax
import jax.numpy as jnp
from jax import lax
from jax.experimental import pallas as pl
from jax.experimental.pallas import tpu as pltpu
from jax.sharding import PartitionSpec as P

HC = 128
CI = 32
KS = 3
STEPS = 2
GATES = 512
KIN = 1440
TAPS = 9

NX = 4
NYL = 2
NZ = 8

BF = jnp.bfloat16
F32 = jnp.float32
MESH = pl.DeviceIdType.MESH

RD = 4
CD = 32
WD = 48
EDGE = 8
ROWS_W = 1536
PARTS = 3
PART = ROWS_W // PARTS
HALF = GATES // 2
BIAS_ROW = TAPS * HC + 3 * CI
SIDES = [(dr, dc) for dr in (-1, 0, 1) for dc in (-1, 0, 1) if (dr, dc) != (0, 0)]


def span(step, halo, size):
    if step == 0:
        return (0, size), (halo, size)
    if step > 0:
        return (size - halo, halo), (0, halo)
    return (0, halo), (halo + size, halo)


def place(x, y, z, core):
    return ((y // NYL) * NX + x, ((y % NYL) * NZ + z) * 2 + core)


def body(
    n_rows,
    n_cols,
    frames_ref,
    hidden_ref,
    cell_ref,
    kernel_ref,
    bias_ref,
    cot_ref,
    hid_out,
    gh_out,
    gc_out,
    total_out,
    hl,
    fl,
    cl,
    kl,
    wp,
    fs,
    x32,
    xb,
    s1,
    s2,
    hs1,
    hs2,
    ga,
    sv,
    c1s,
    dcs,
    dg2,
    dg1,
    dgo,
    zs,
    a0,
    o0,
    r0,
    a1,
    r1z,
    r1y,
    r1x,
    a2z,
    a2y,
    a2x,
    r2z,
    r2y,
    r2x,
    r3z,
    r3y,
    r3x,
    gs,
    halo_send,
    halo_recv,
    loc_sem,
    st_send,
    st_recv,
):
    r = lax.axis_index("rows")
    c = lax.axis_index("cols")
    ny = (n_rows // NX) * NYL
    x = lax.rem(r, NX)
    core = lax.rem(c, 2)
    z = lax.rem(c // 2, NZ)
    y = (r // NX) * NYL + c // (2 * NZ)
    size = {"x": NX, "y": ny, "z": NZ}
    mine = {"x": x, "y": y, "z": z}

    def peer(axis, d):
        at = dict(mine)
        at[axis] = lax.rem(mine[axis] + d, size[axis])
        return place(at["x"], at["y"], at["z"], core)

    sibling = place(x, y, z, 1 - core)

    def neighbour(dr, dc):
        return (lax.rem(r + dr + n_rows, n_rows), lax.rem(c + dc + n_cols, n_cols))

    barrier = pltpu.get_barrier_semaphore()
    greet = [neighbour(dr, dc) for dr, dc in SIDES] + [sibling]
    for axis in ("x", "y", "z"):
        greet += [peer(axis, d) for d in range(1, size[axis])]
    for who in greet:
        pl.semaphore_signal(barrier, inc=1, device_id=who, device_id_type=MESH)

    local = []

    def fetch(src, dst):
        copy = pltpu.make_async_copy(src, dst, loc_sem.at[len(local)])
        copy.start()
        local.append(copy)

    fetch(hidden_ref, hl.at[pl.ds(4, RD), pl.ds(16, CD), :])
    fetch(frames_ref, fl.at[1, :, :, pl.ds(128, CD * CI)])
    fetch(cell_ref, cl.at[pl.ds(3, RD), pl.ds(8, CD), :])
    fetch(cot_ref, kl.at[:, pl.ds(2, RD), pl.ds(16, CD), :])
    for tap in range(TAPS):
        a, b = divmod(tap, KS)
        fetch(kernel_ref.at[pl.ds(tap * 160 + CI, HC), :], wp.at[pl.ds(tap * HC, HC), :])
        fetch(
            kernel_ref.at[pl.ds(tap * 160, CI), :],
            wp.at[pl.ds(TAPS * HC + a * 128 + b * CI, CI), :],
        )
    pl.semaphore_wait(barrier, len(greet))

    halos = []
    for i, (dr, dc) in enumerate(SIDES):
        who = neighbour(dr, dc)

        def send(kind, src, dst):
            copy = pltpu.make_async_remote_copy(
                src_ref=src,
                dst_ref=dst,
                send_sem=halo_send.at[i, kind],
                recv_sem=halo_recv.at[i, kind],
                device_id=who,
                device_id_type=MESH,
            )
            copy.start()
            halos.append(copy)

        (rs, rn), (rt, _) = span(dr, 4, RD)
        (cs, cn), (ct, _) = span(dc, 16, CD)
        send(
            0,
            hidden_ref.at[pl.ds(rs, rn), pl.ds(cs, cn), :],
            hl.at[pl.ds(rt, rn), pl.ds(ct, cn), :],
        )
        (ls, ln), (lt, _) = span(dc, 128, CD * CI)
        send(1, frames_ref.at[:, :, pl.ds(ls, ln)], fl.at[1 - dr, :, :, pl.ds(lt, ln)])
        (rs, rn), (rt, _) = span(dr, 3, RD)
        (cs, cn), (ct, _) = span(dc, 8, CD)
        send(
            2,
            cell_ref.at[pl.ds(rs, rn), pl.ds(cs, cn), :],
            cl.at[pl.ds(rt, rn), pl.ds(ct, cn), :],
        )
        (rs, rn), (rt, _) = span(dr, 2, RD)
        (cs, cn), (ct, _) = span(dc, 16, CD)
        send(
            3,
            cot_ref.at[:, pl.ds(rs, rn), pl.ds(cs, cn), :],
            kl.at[:, pl.ds(rt, rn), pl.ds(ct, cn), :],
        )

    for a in range(KS):
        wp[pl.ds(TAPS * HC + a * 128 + 96, 32), :] = jnp.zeros((32, GATES), BF)
    x32[...] = jnp.zeros_like(x32)
    edge = jnp.zeros((EDGE, HC), F32)
    s1[pl.ds(0, EDGE), :] = edge
    s1[pl.ds(EDGE + 12 * WD, EDGE), :] = edge
    s2[pl.ds(0, EDGE), :] = edge
    s2[pl.ds(EDGE + 10 * WD, EDGE), :] = edge
    wide = jnp.zeros((EDGE, TAPS * HC), F32)
    zs[pl.ds(0, EDGE), :] = wide
    zs[pl.ds(EDGE + 8 * WD, EDGE), :] = wide
    fs[...] = jnp.zeros_like(fs)

    at_col = lax.broadcasted_iota(jnp.int32, (WD, HC), 0) - 8
    in_raster = (at_col + c * CD >= 0) & (at_col + c * CD < n_cols * CD)
    col_mask = jnp.where(in_raster, 1.0, 0.0).astype(F32)
    own_mask = jnp.where((at_col >= 0) & (at_col < CD), 1.0, 0.0).astype(F32)

    def row_mask(row):
        there = r * RD + row
        inside = (there >= 0) & (there < n_rows * RD)
        return col_mask * jnp.where(inside, 1.0, 0.0).astype(F32)

    lane = lax.broadcasted_iota(jnp.int32, (16, 1280), 1)
    line = lax.broadcasted_iota(jnp.int32, (16, 1280), 0)
    there_col = lane // CI - 4 + c * CD
    there_row = line - 4 + r * RD
    frame_mask = jnp.where(
        (there_col >= 0)
        & (there_col < n_cols * CD)
        & (there_row >= 0)
        & (there_row < n_rows * RD),
        1.0,
        0.0,
    ).astype(F32)

    for copy in local:
        copy.wait()
    for copy in halos:
        copy.wait_recv()

    for row in range(12):
        vals = hl[row].astype(F32)[8 : 8 + WD, :]
        s1[pl.ds(EDGE + row * WD, WD), :] = vals * row_mask(row - 4)
    for b in range(KS):
        hs1[b] = s1[pl.ds(EDGE + b - 1, 12 * WD), :].astype(BF)
    low = lax.broadcasted_iota(jnp.int32, (12, HC), 1) < CI
    ones = jnp.where(
        lax.broadcasted_iota(jnp.int32, (WD, HC), 1) == 3 * CI, 1.0, 0.0
    ).astype(F32)
    for t in range(STEPS):
        for k in range(3):
            fs[t, pl.ds(4 * k, 4), :] = fl[k, t].astype(F32)
        for g in range(10):
            vals = fs[t, pl.ds(0, 12), pl.ds(g * 128, 128)] * frame_mask[:12, g * 128 : (g + 1) * 128]
            for j in range(4):
                turned = vals if j == 0 else pltpu.roll(vals, 128 - 32 * j, 1)
                x32[t, pl.ds(EDGE + 4 + 4 * g + j, 12, stride=WD), :] = jnp.where(low, turned, 0.0)
        for row in range(12):
            at = EDGE + row * WD
            joined = (
                x32[t, pl.ds(at - 1, WD), :]
                + pltpu.roll(x32[t, pl.ds(at, WD), :], 32, 1)
                + pltpu.roll(x32[t, pl.ds(at + 1, WD), :], 64, 1)
                + ones
            )
            xb[t, pl.ds(row * WD, WD), :] = joined.astype(BF)

    bias = bias_ref[...]

    def gates_of(hs, t, first, count):
        size_m = count * WD
        blocks = [
            hs[b, pl.ds(a * WD, size_m), :] for a in range(KS) for b in range(KS)
        ] + [xb[t, pl.ds((first + a) * WD, size_m), :] for a in range(KS)]
        lhs = jnp.concatenate(blocks, axis=1)
        ga[pl.ds(0, size_m), :] = jnp.dot(lhs, wp[...], preferred_element_type=F32)

    def sigmoid(v):
        return 0.5 * jnp.tanh(0.5 * v) + 0.5

    def activated(row):
        pre = ga[pl.ds(row * WD, WD), :] + bias
        return (
            sigmoid(pre[:, :HC]),
            sigmoid(pre[:, HC : 2 * HC]),
            jnp.tanh(pre[:, 2 * HC : 3 * HC]),
            sigmoid(pre[:, 3 * HC :]),
        )

    gates_of(hs1, 0, 0, 10)
    for k in range(10):
        row = k - 3
        gi, gf, gg, go = activated(k)
        now = gf * cl[k] + gi * gg
        th = jnp.tanh(now)
        c1s[pl.ds(k * WD, WD), :] = now
        if -1 <= row <= 4:
            at = pl.ds((row + 1) * WD, WD)
            for q, val in enumerate((gi, gf, gg, go, th)):
                sv[q, at, :] = val
        h = (go * th).astype(BF).astype(F32)
        s2[pl.ds(EDGE + k * WD, WD), :] = h * row_mask(row)
    for b in range(KS):
        hs2[b] = s2[pl.ds(EDGE + b - 1, 10 * WD), :].astype(BF)

    gates_of(hs2, 1, 1, 8)

    def backward(k, row, s, dh, gi, gf, gg, go, th, before, dg, own_at):
        mask = row_mask(row)
        pres = (
            s * gg * gi * (1.0 - gi),
            s * before * gf * (1.0 - gf),
            s * gi * (1.0 - gg * gg),
            dh * th * go * (1.0 - go),
        )
        for q, pre in enumerate(pres):
            cols = pl.ds(q * HC, HC)
            masked = pre * mask
            dg[pl.ds(k * WD, WD), cols] = masked.astype(BF)
            if 0 <= row < RD:
                dgo[pl.ds(own_at + row * WD, WD), cols] = (masked * own_mask).astype(BF)

    for k in range(8):
        row = k - 2
        gi, gf, gg, go = activated(k)
        before = c1s[pl.ds((k + 1) * WD, WD), :]
        now = gf * before + gi * gg
        th = jnp.tanh(now)
        if 0 <= row < RD:
            hid_out[row] = (go * th)[8 : 8 + CD, :].astype(BF)
        dh = kl[1, k].astype(F32)[8 : 8 + WD, :]
        s = dh * go * (1.0 - th * th)
        if -1 <= row <= 4:
            dcs[pl.ds((row + 1) * WD, WD), :] = s * gf
        backward(k, row, s, dh, gi, gf, gg, go, th, before, dg2, RD * WD)

    def adjoint(dg, count):
        size_m = count * WD
        zs[pl.ds(EDGE, size_m), :] = lax.dot_general(
            dg[pl.ds(0, size_m), :],
            wp[pl.ds(0, TAPS * HC), :],
            (((1,), (1,)), ((), ())),
            preferred_element_type=F32,
        )

    def gathered(k):
        total = None
        for tap in range(TAPS):
            a, b = divmod(tap, KS)
            term = zs[pl.ds(EDGE + (k + 2 - a) * WD - (b - 1), WD), pl.ds(tap * HC, HC)]
            total = term if total is None else total + term
        return total

    adjoint(dg2, 8)
    for k in range(6):
        row = k - 1
        at = pl.ds(k * WD, WD)
        gi, gf, gg, go, th = (sv[q, at, :] for q in range(5))
        dh = gathered(k) + kl[0, k + 1].astype(F32)[8 : 8 + WD, :]
        s = dcs[at, :] + dh * go * (1.0 - th * th)
        if 0 <= row < RD:
            gc_out[row] = (s * gf)[8 : 8 + CD, :]
        backward(k, row, s, dh, gi, gf, gg, go, th, cl[k + 2], dg1, 0)

    count = [0]

    def copy_to(src, dst, who):
        i = count[0]
        count[0] += 1
        return pltpu.make_async_remote_copy(
            src_ref=src,
            dst_ref=dst,
            send_sem=st_send.at[i],
            recv_sem=st_recv.at[i],
            device_id=who,
            device_id_type=MESH,
        )

    sent = []
    mine_at = pl.multiple_of(core * HALF, HALF)
    other_at = pl.multiple_of((1 - core) * HALF, HALF)

    def weight_blocks(p):
        blocks = []
        for q in range(4 * p, 4 * p + 4):
            if q < TAPS:
                a, b = divmod(q, KS)
                one = hs1[b, pl.ds((3 + a) * WD, RD * WD), :]
                two = hs2[b, pl.ds((2 + a) * WD, RD * WD), :]
            else:
                a = q - TAPS
                one = xb[0, pl.ds((3 + a) * WD, RD * WD), :]
                two = xb[1, pl.ds((3 + a) * WD, RD * WD), :]
            blocks.append(jnp.concatenate([one, two], axis=0))
        return jnp.concatenate(blocks, axis=1)

    swaps = []
    for p in range(PARTS):
        lhs = weight_blocks(p)
        dims = (((0,), (0,)), ((), ()))
        a0[p] = lax.dot_general(
            lhs, dgo[:, pl.ds(other_at, HALF)], dims, preferred_element_type=F32
        ).astype(BF)
        copy = copy_to(a0.at[p], r0.at[p], sibling)
        copy.start()
        swaps.append(copy)
        o0[p] = lax.dot_general(
            lhs, dgo[:, pl.ds(mine_at, HALF)], dims, preferred_element_type=F32
        )
    sent += swaps

    adjoint(dg1, 6)
    for row in range(RD):
        gh_out[row] = gathered(row)[8 : 8 + CD, :]

    plans = [
        ("z", "y", "x", r1z, a2z, r2z, r3z),
        ("y", "z", "x", r1y, a2y, r2y, r3y),
        ("x", "z", "y", r1x, a2x, r2x, r3x),
    ]
    state = []
    for p, (ax1, ax2, ax3, r1, a2, r2, r3) in enumerate(plans):
        n1, n2, n3 = size[ax1], size[ax2], size[ax3]
        rows1 = PART // n1
        rows2 = rows1 // n2
        if rows2 >= 16:
            unit = (rows2, HALF)
        else:
            unit = (16, HALF * rows2 // 16)
        across = HALF // unit[1]

        def unit_at(u, unit=unit, across=across):
            return (
                pl.multiple_of((u // across) * unit[0], 16),
                pl.multiple_of(lax.rem(u, across) * unit[1], 128),
            )

        state.append((n1, n2, n3, rows1, unit, unit_at))

    stage1 = []
    for p, (ax1, ax2, ax3, r1, a2, r2, r3) in enumerate(plans):
        n1, n2, n3, rows1, unit, unit_at = state[p]
        swaps[p].wait_recv()
        a1[p] = (o0[p] + r0[p].astype(F32)).astype(BF)
        copies = []
        for d in range(1, n1):
            to = lax.rem(mine[ax1] + d, n1)
            copy = copy_to(
                a1.at[p, pl.ds(pl.multiple_of(to * rows1, 16), rows1), :],
                r1.at[d - 1],
                peer(ax1, d),
            )
            copy.start()
            copies.append(copy)
        stage1.append(copies)
        sent += copies

    stage2 = []
    for p, (ax1, ax2, ax3, r1, a2, r2, r3) in enumerate(plans):
        n1, n2, n3, rows1, unit, unit_at = state[p]
        for copy in stage1[p]:
            copy.wait_recv()
        at = pl.ds(pl.multiple_of(mine[ax1] * rows1, 16), rows1)
        total = a1[p, at, :].astype(F32)
        for d in range(1, n1):
            total = total + r1[d - 1].astype(F32)
        a2[...] = total.astype(BF)
        copies = []
        for d in range(1, n2):
            ur, uc = unit_at(lax.rem(mine[ax2] + d, n2))
            copy = copy_to(
                a2.at[pl.ds(ur, unit[0]), pl.ds(uc, unit[1])], r2.at[d - 1], peer(ax2, d)
            )
            copy.start()
            copies.append(copy)
        stage2.append(copies)
        sent += copies

    stage3 = []
    for p, (ax1, ax2, ax3, r1, a2, r2, r3) in enumerate(plans):
        n1, n2, n3, rows1, unit, unit_at = state[p]
        for copy in stage2[p]:
            copy.wait_recv()
        ur, uc = unit_at(mine[ax2])
        total = a2[pl.ds(ur, unit[0]), pl.ds(uc, unit[1])].astype(F32)
        for d in range(1, n2):
            total = total + r2[d - 1].astype(F32)
        r3[mine[ax3]] = total.astype(BF)
        copies = []
        for d in range(1, n3):
            copy = copy_to(r3.at[mine[ax3]], r3.at[mine[ax3]], peer(ax3, d))
            copy.start()
            copies.append(copy)
        stage3.append(copies)
        sent += copies

    stage4 = []
    for p, (ax1, ax2, ax3, r1, a2, r2, r3) in enumerate(plans):
        n1, n2, n3, rows1, unit, unit_at = state[p]
        for copy in stage3[p]:
            copy.wait_recv()
        total = r3[0].astype(F32)
        for d in range(1, n3):
            total = total + r3[d].astype(F32)
        ur, uc = unit_at(mine[ax2])
        slot = gs.at[
            pl.ds(pl.multiple_of(p * PART + mine[ax1] * rows1 + ur, 16), unit[0]),
            pl.ds(pl.multiple_of(mine_at + uc, 128), unit[1]),
        ]
        slot[...] = total.astype(BF)
        copies = []
        for d in range(1, n2):
            copy = copy_to(slot, slot, peer(ax2, d))
            copy.start()
            copies.append(copy)
        stage4.append(copies)
        sent += copies

    stage5 = []
    for p, (ax1, ax2, ax3, r1, a2, r2, r3) in enumerate(plans):
        n1, n2, n3, rows1, unit, unit_at = state[p]
        for copy in stage4[p]:
            copy.wait_recv()
        slot = gs.at[
            pl.ds(pl.multiple_of(p * PART + mine[ax1] * rows1, 16), rows1),
            pl.ds(mine_at, HALF),
        ]
        copies = []
        for d in range(1, n1):
            copy = copy_to(slot, slot, peer(ax1, d))
            copy.start()
            copies.append(copy)
        stage5.append(copies)
        sent += copies

    stage6 = []
    for p in range(PARTS):
        for copy in stage5[p]:
            copy.wait_recv()
        slot = gs.at[pl.ds(p * PART, PART), pl.ds(mine_at, HALF)]
        copy = copy_to(slot, slot, sibling)
        copy.start()
        stage6.append(copy)
    sent += stage6
    for copy in stage6:
        copy.wait_recv()

    for tap in range(TAPS):
        a, b = divmod(tap, KS)
        total_out[pl.ds(tap * 160, CI), :] = gs[
            pl.ds(TAPS * HC + a * 128 + b * CI, CI), :
        ]
        total_out[pl.ds(tap * 160 + CI, HC), :] = gs[pl.ds(tap * HC, HC), :]
    total_out[pl.ds(KIN, 16), :] = gs[pl.ds(BIAS_ROW, 16), :]

    for copy in halos:
        copy.wait_send()
    for copy in sent:
        copy.wait_send()


def units(n1, n2):
    rows1 = PART // n1
    rows2 = rows1 // n2
    return (rows2, HALF) if rows2 >= 16 else (16, HALF * rows2 // 16)


def shards(frames, hidden_start, cell_start, kernel, gate_bias, cotangent):
    n_rows = lax.axis_size("rows")
    n_cols = lax.axis_size("cols")
    ny = (n_rows // NX) * NYL
    uz = units(NZ, ny)
    uy = units(ny, NZ)
    ux = units(NX, NZ)
    vmem = pltpu.VMEM
    scratch = [
        vmem((12, 64, HC), BF),
        vmem((3, STEPS, RD, 1280), BF),
        vmem((10, WD, HC), F32),
        vmem((STEPS, 8, 64, HC), BF),
        vmem((ROWS_W, GATES), BF),
        vmem((STEPS, 16, 1280), F32),
        vmem((STEPS, 12 * WD + 2 * EDGE, HC), F32),
        vmem((STEPS, 12 * WD, HC), BF),
        vmem((12 * WD + 2 * EDGE, HC), F32),
        vmem((10 * WD + 2 * EDGE, HC), F32),
        vmem((KS, 12 * WD, HC), BF),
        vmem((KS, 10 * WD, HC), BF),
        vmem((10 * WD, GATES), F32),
        vmem((5, 6 * WD, HC), F32),
        vmem((10 * WD, HC), F32),
        vmem((6 * WD, HC), F32),
        vmem((8 * WD, GATES), BF),
        vmem((6 * WD, GATES), BF),
        vmem((2 * RD * WD, GATES), BF),
        vmem((8 * WD + 2 * EDGE, TAPS * HC), F32),
        vmem((PARTS, PART, HALF), BF),
        vmem((PARTS, PART, HALF), F32),
        vmem((PARTS, PART, HALF), BF),
        vmem((PARTS, PART, HALF), BF),
        vmem((NZ - 1, PART // NZ, HALF), BF),
        vmem((ny - 1, PART // ny, HALF), BF),
        vmem((NX - 1, PART // NX, HALF), BF),
        vmem((PART // NZ, HALF), BF),
        vmem((PART // ny, HALF), BF),
        vmem((PART // NX, HALF), BF),
        vmem((ny - 1,) + uz, BF),
        vmem((NZ - 1,) + uy, BF),
        vmem((NZ - 1,) + ux, BF),
        vmem((NX,) + uz, BF),
        vmem((NX,) + uy, BF),
        vmem((ny,) + ux, BF),
        vmem((ROWS_W, GATES), BF),
        pltpu.SemaphoreType.DMA((8, 4)),
        pltpu.SemaphoreType.DMA((8, 4)),
        pltpu.SemaphoreType.DMA((22,)),
        pltpu.SemaphoreType.DMA((stages(n_rows),)),
        pltpu.SemaphoreType.DMA((stages(n_rows),)),
    ]
    anywhere = pl.BlockSpec(memory_space=pl.ANY)
    in_vmem = pl.BlockSpec(memory_space=pltpu.VMEM)
    hidden, grad_hidden, grad_cell, total = pl.pallas_call(
        functools.partial(body, n_rows, n_cols),
        out_shape=(
            jax.ShapeDtypeStruct((RD, CD, HC), BF),
            jax.ShapeDtypeStruct((RD, CD, HC), F32),
            jax.ShapeDtypeStruct((RD, CD, HC), F32),
            jax.ShapeDtypeStruct((KIN + 16, GATES), BF),
        ),
        in_specs=[anywhere, anywhere, anywhere, anywhere, in_vmem, anywhere],
        out_specs=(in_vmem, in_vmem, in_vmem, in_vmem),
        scratch_shapes=scratch,
        compiler_params=pltpu.CompilerParams(
            collective_id=0, has_side_effects=True, vmem_limit_bytes=48 * 1024 * 1024
        ),
    )(frames, hidden_start, cell_start, kernel, gate_bias.reshape(1, GATES), cotangent)
    scale = 1.0 / math.sqrt(STEPS * n_rows * RD * n_cols * CD)
    kernel_grad = total[:KIN].astype(F32) * scale
    bias_grad = total[KIN].astype(F32) * scale
    return hidden, grad_hidden, grad_cell, kernel_grad, bias_grad


def stages(n_rows):
    ny = (n_rows // NX) * NYL
    one = (NZ - 1) + (ny - 1) + (NX - 1)
    two = (ny - 1) + (NZ - 1) + (NZ - 1)
    three = (NX - 1) + (NX - 1) + (ny - 1)
    return 2 * PARTS + 2 * one + 2 * two + three


def solution(mesh):
    placed = (
        P(None, "rows", "cols"),
        P("rows", "cols", None),
        P("rows", "cols", None),
        P(),
        P(),
        P(None, "rows", "cols", None),
    )
    return jax.shard_map(
        shards,
        mesh=mesh,
        in_specs=placed,
        out_specs=(
            P("rows", "cols", None),
            P("rows", "cols", None),
            P("rows", "cols", None),
            P(),
            P(),
        ),
        check_vma=False,
    )
```

time: 498 us -> 79.7 us (0.16)
  waiting for transfers between devices: 284 us -> 0 us
  blocking collectives: 120 us -> 0 us
  Pallas kernels: 0 us -> 69 us
  starting transfers between devices: 50.3 us -> 0 us
  between operations: 14.7 us -> 0.66 us
  other arithmetic: 9.55 us -> 2.62 us
  matrix products: 5.7 us -> 0 us
  local copies, waits for them, and re-layouts: 12.7 us -> 7.07 us
    psum x1 -> x0, waiting for transfers between devices: 272 us -> none  [shards(): lax.psum((kernel_acc, bias_acc), ('rows', 'cols'))]
    psum x1 -> x0, blocking collectives: 120 us -> none  [shards(): lax.psum((kernel_acc, bias_acc), ('rows', 'cols'))]
    pallas_call x0 -> x1, Pallas kernels: none -> 69 us  [shards(): pl.pallas_call(functools.partial(body, n_rows, n_cols), out_shape=(jax.Sh...]
    ppermute x16 -> x0, starting transfers between devices: 50.2 us -> none  [the longest x8 30.6 us: extended(): lax.ppermute(tail, axis, [(i, (i + 1) % count) for i in range(ends)])]
    ppermute x16 -> x0, waiting for transfers between devices: 12.1 us -> none  [the longest x8 11.3 us: extended(): lax.ppermute(head, axis, [((i + 1) % count, i) for i in range(ends)])]
    reshape x2 -> x0, local copies, waits for them, and re-layouts: 6.41 us -> none  [the longest x1 3.95 us: shards(): jnp.transpose(blocks, (0, 2, 1)).reshape(taps * GATES, chans)]
    dot_general x6 -> x0, matrix products: 5.7 us -> none  [the longest x2 2.74 us: shards(): jnp.dot(patches.T, flat_grads, preferred_element_type=jnp.float32)]
  transfers between devices with their start and end apart: 17 -> 0, of which waited for: 7 -> 0; matrix products, arithmetic and copies ran while one was open for 3% -> 0% of each run, Pallas kernels for 0% -> 0%
where the time goes in v1:
time: 79.7 us; the launch traced here: 79.3 us
  Pallas kernels  69 us (87%)
  local copies, waits for them, and re-layouts  7.07 us (9%)
  other arithmetic  2.62 us (3%)
    pallas_call x1, Pallas kernels, shards(): pl.pallas_call(functools.partial(body, n_rows, n_cols), out_shape=(jax.Sh...  69 us
    unnamed x15, local copies, waits for them, and re-layouts  7.07 us
    mul x1, other arithmetic, shards(): kernel_grad = total[:KIN].astype(F32) * scale  2.04 us

profile of v1, /device:TPU:1, one launch (start us, length us, event | category | flops | bytes accessed | tf_op | source)
XLA Modules:
  0.0 79.3 jit_solution(14270629057522619824)
XLA Ops:
  0.6 0.0 copy-start
  0.6 1.4 %copy-done = bf16[1440,512]{1,0:T(8,128)(2,1)S(1)} copy-done((bf16[1440,512]{1,0:T(8,128)(2,1)S(1)}, bf16[1440,512]{1,0:T(8,128)(2,1)}, u32[]{:S(2)}) %copy-start) | copy-done | bytes 1474584
  2.0 0.0 copy-start.1
  2.0 0.8 %copy-done.1 = f32[4,32,128]{2,1,0:T(8,128)S(1)} copy-done((f32[4,32,128]{2,1,0:T(8,128)S(1)}, f32[4,32,128]{2,1,0:T(8,128)}, u32[]{:S(2)}) %copy-start.1) | copy-done | bytes 65560
  2.8 0.0 copy-start.2
  2.8 0.8 %copy-done.2 = bf16[2,4,32,128]{3,2,1,0:T(8,128)(2,1)S(1)} copy-done((bf16[2,4,32,128]{3,2,1,0:T(8,128)(2,1)S(1)}, bf16[2,4,32,128]{3,2,1,0:T(8,128)(2,1)}, u32[]{:S(2)}) %copy-start.2) | copy-done | bytes 65560
  3.7 0.0 copy-start.3
  3.7 0.8 copy-done.3
  4.4 0.0 copy-start.4
  4.4 0.7 copy-done.4
  5.2 0.0 copy-start.5
  5.2 0.7 copy-done.5
  5.8 69.0 %shard_map.101 = (bf16[4,32,128]{2,1,0:T(8,128)(2,1)S(1)}, f32[4,32,128]{2,1,0:T(8,128)S(1)}, f32[4,32,128]{2,1,0:T(8,128)S(1)}, bf16[1456,512]{1,0:T(8,128)(2,1)S(1)}) custom-call(bf16[2,4,1024]{2,1,0:T(4,128)(2,1)S(1)} %copy-done.4, bf16[4,32,128]{2,1,0:T(8,128)(2,1)S(1)} %copy-done.3, f32[4,32,128]{2,1,0:T(8,128)S(1)} %copy-done.1, ...), custom_call_target="tpu_custom_call" | custom-call | tf_op jit(solution)/shard_map/pallas_call | solution.py:616
  74.8 0.6 convert_multiply_fusion.1
  75.4 2.0 %convert_multiply_fusion = f32[1440,512]{1,0:T(8,128)} fusion(bf16[1456,512]{1,0:T(8,128)(2,1)S(1)} %get-tuple-element.12), kind=kLoop, calls=%fused_computation | loop fusion | flops 1474560 | bytes 4423680 | tf_op jit(solution)/shard_map/mul | solution.py:632
  77.4 0.6 copy.14
  78.0 0.6 copy.15
  78.7 0.6 copy.16
Async XLA Ops:
  0.6 1.4 %copy-start = (bf16[1440,512]{1,0:T(8,128)(2,1)S(1)}, bf16[1440,512]{1,0:T(8,128)(2,1)}, u32[]{:S(2)}) copy-start(bf16[1440,512]{1,0:T(8,128)(2,1)} %kernel_ref.1) | copy-start | bytes 4423684
  2.0 0.8 %copy-start.1 = (f32[4,32,128]{2,1,0:T(8,128)S(1)}, f32[4,32,128]{2,1,0:T(8,128)}, u32[]{:S(2)}) copy-start(f32[4,32,128]{2,1,0:T(8,128)} %cell_ref.1) | copy-start | bytes 196612
  2.8 0.8 %copy-start.2 = (bf16[2,4,32,128]{3,2,1,0:T(8,128)(2,1)S(1)}, bf16[2,4,32,128]{3,2,1,0:T(8,128)(2,1)}, u32[]{:S(2)}) copy-start(bf16[2,4,32,128]{3,2,1,0:T(8,128)(2,1)} %cot_ref.1) | copy-start | bytes 196612
  3.7 0.8 copy-start.3
  4.4 0.7 copy-start.4
  5.2 0.7 copy-start.5

commit v2 on v1

--- a/solution.py
+++ b/solution.py
@@ -61,11 +61,17 @@
     gh_out,
     gc_out,
     total_out,
-    hl,
+    hown,
     fl,
-    cl,
-    kl,
+    cown,
+    kown,
     wp,
+    ud,
+    st,
+    co,
+    ud_in,
+    st_in,
+    co_in,
     fs,
     x32,
     xb,
@@ -75,12 +81,17 @@
     hs2,
     ga,
     sv,
+    c0s,
     c1s,
+    k1s,
     dcs,
     dg2,
-    dg1,
     dgo,
     zs,
+    cb,
+    ud_c,
+    lr_c,
+    co_c,
     a0,
     o0,
     r0,
@@ -100,6 +111,8 @@
     gs,
     halo_send,
     halo_recv,
+    late_send,
+    late_recv,
     loc_sem,
     st_send,
     st_recv,
@@ -138,10 +151,10 @@
         copy.start()
         local.append(copy)
 
-    fetch(hidden_ref, hl.at[pl.ds(4, RD), pl.ds(16, CD), :])
+    fetch(hidden_ref, hown)
+    fetch(cell_ref, cown)
+    fetch(cot_ref, kown)
     fetch(frames_ref, fl.at[1, :, :, pl.ds(128, CD * CI)])
-    fetch(cell_ref, cl.at[pl.ds(3, RD), pl.ds(8, CD), :])
-    fetch(cot_ref, kl.at[:, pl.ds(2, RD), pl.ds(16, CD), :])
     for tap in range(TAPS):
         a, b = divmod(tap, KS)
         fetch(kernel_ref.at[pl.ds(tap * 160 + CI, HC), :], wp.at[pl.ds(tap * HC, HC), :])
@@ -149,13 +162,50 @@
             kernel_ref.at[pl.ds(tap * 160, CI), :],
             wp.at[pl.ds(TAPS * HC + a * 128 + b * CI, CI), :],
         )
+    for copy in local[:3]:
+        copy.wait()
+    fields = (
+        ([hown[i] for i in range(RD)], 3),
+        ([cown[i] for i in range(RD)], 2),
+        ([kown[1, i] for i in range(RD)], 1),
+    )
+
+    def edge_rows(step, depth):
+        if step == 0:
+            return range(RD)
+        return range(depth) if step < 0 else range(RD - depth, RD)
+
+    def outgoing(dr, dc):
+        pieces = []
+        for rows, depth in fields:
+            for i in edge_rows(dr, depth):
+                piece = rows[i].astype(F32)
+                if dc != 0:
+                    piece = piece[:8, :] if dc < 0 else piece[CD - 8 :, :]
+                pieces.append(piece)
+        return jnp.concatenate(pieces, axis=0).astype(BF)
+
+    def slot_of(dr, dc, rows_buf, sides_buf, corners_buf):
+        if dc == 0:
+            return rows_buf.at[(dr + 1) // 2]
+        if dr == 0:
+            return sides_buf.at[(dc + 1) // 2]
+        return corners_buf.at[(dr + 1) + (dc + 1) // 2]
+
+    for dr, dc in SIDES:
+        slot_of(dr, dc, ud, st, co)[...] = outgoing(dr, dc)
     pl.semaphore_wait(barrier, len(greet))
 
     halos = []
     for i, (dr, dc) in enumerate(SIDES):
         who = neighbour(dr, dc)
-
-        def send(kind, src, dst):
+        (ls, ln), (lt, _) = span(dc, 128, CD * CI)
+        for kind, (src, dst) in enumerate(
+            (
+                (slot_of(dr, dc, ud, st, co), slot_of(dr, dc, ud_in, st_in, co_in)),
+                (frames_ref.at[:, :, pl.ds(ls, ln)], fl.at[1 - dr, :, :, pl.ds(lt, ln)]),
+            )
+        ):
             copy = pltpu.make_async_remote_copy(
                 src_ref=src,
                 dst_ref=dst,
@@ -167,41 +217,17 @@
             copy.start()
             halos.append(copy)
 
-        (rs, rn), (rt, _) = span(dr, 4, RD)
-        (cs, cn), (ct, _) = span(dc, 16, CD)
-        send(
-            0,
-            hidden_ref.at[pl.ds(rs, rn), pl.ds(cs, cn), :],
-            hl.at[pl.ds(rt, rn), pl.ds(ct, cn), :],
-        )
-        (ls, ln), (lt, _) = span(dc, 128, CD * CI)
-        send(1, frames_ref.at[:, :, pl.ds(ls, ln)], fl.at[1 - dr, :, :, pl.ds(lt, ln)])
-        (rs, rn), (rt, _) = span(dr, 3, RD)
-        (cs, cn), (ct, _) = span(dc, 8, CD)
-        send(
-            2,
-            cell_ref.at[pl.ds(rs, rn), pl.ds(cs, cn), :],
-            cl.at[pl.ds(rt, rn), pl.ds(ct, cn), :],
-        )
-        (rs, rn), (rt, _) = span(dr, 2, RD)
-        (cs, cn), (ct, _) = span(dc, 16, CD)
-        send(
-            3,
-            cot_ref.at[:, pl.ds(rs, rn), pl.ds(cs, cn), :],
-            kl.at[:, pl.ds(rt, rn), pl.ds(ct, cn), :],
-        )
-
     for a in range(KS):
         wp[pl.ds(TAPS * HC + a * 128 + 96, 32), :] = jnp.zeros((32, GATES), BF)
     x32[...] = jnp.zeros_like(x32)
     edge = jnp.zeros((EDGE, HC), F32)
     s1[pl.ds(0, EDGE), :] = edge
-    s1[pl.ds(EDGE + 12 * WD, EDGE), :] = edge
+    s1[pl.ds(EDGE + 10 * WD, EDGE), :] = edge
     s2[pl.ds(0, EDGE), :] = edge
-    s2[pl.ds(EDGE + 10 * WD, EDGE), :] = edge
+    s2[pl.ds(EDGE + 8 * WD, EDGE), :] = edge
     wide = jnp.zeros((EDGE, TAPS * HC), F32)
     zs[pl.ds(0, EDGE), :] = wide
-    zs[pl.ds(EDGE + 8 * WD, EDGE), :] = wide
+    zs[pl.ds(EDGE + 6 * WD, EDGE), :] = wide
     fs[...] = jnp.zeros_like(fs)
 
     at_col = lax.broadcasted_iota(jnp.int32, (WD, HC), 0) - 8
@@ -227,16 +253,39 @@
         0.0,
     ).astype(F32)
 
-    for copy in local:
+    for copy in local[3:]:
         copy.wait()
     for copy in halos:
         copy.wait_recv()
 
-    for row in range(12):
-        vals = hl[row].astype(F32)[8 : 8 + WD, :]
-        s1[pl.ds(EDGE + row * WD, WD), :] = vals * row_mask(row - 4)
+    def incoming(dr, dc):
+        return slot_of(-dr, -dc, ud_in, st_in, co_in)[...].astype(F32)
+
+    around = {side: incoming(*side) for side in SIDES}
+
+    def field_row(which, row):
+        rows, depth = fields[which]
+        before = [d for _, d in fields[:which]]
+        dr = -1 if row < 0 else (1 if row >= RD else 0)
+        i = row + depth if row < 0 else (row - RD if row >= RD else row)
+        parts = []
+        for dc in (-1, 0, 1):
+            if (dr, dc) == (0, 0):
+                parts.append(rows[row].astype(F32))
+                continue
+            wide_row = CD if dc == 0 else 8
+            skip = (RD * which if dr == 0 else sum(before)) * wide_row
+            parts.append(around[dr, dc][skip + i * wide_row : skip + (i + 1) * wide_row, :])
+        return jnp.concatenate(parts, axis=0)
+
+    for k in range(10):
+        s1[pl.ds(EDGE + k * WD, WD), :] = field_row(0, k - 3) * row_mask(k - 3)
+    for k in range(8):
+        c0s[pl.ds(k * WD, WD), :] = field_row(1, k - 2)
+    for k in range(6):
+        k1s[pl.ds(k * WD, WD), :] = field_row(2, k - 1)
     for b in range(KS):
-        hs1[b] = s1[pl.ds(EDGE + b - 1, 12 * WD), :].astype(BF)
+        hs1[b] = s1[pl.ds(EDGE + b - 1, 10 * WD), :].astype(BF)
     low = lax.broadcasted_iota(jnp.int32, (12, HC), 1) < CI
     ones = jnp.where(
         lax.broadcasted_iota(jnp.int32, (WD, HC), 1) == 3 * CI, 1.0, 0.0
@@ -281,52 +330,49 @@
             sigmoid(pre[:, 3 * HC :]),
         )
 
-    gates_of(hs1, 0, 0, 10)
-    for k in range(10):
-        row = k - 3
+    gates_of(hs1, 0, 1, 8)
+    for k in range(8):
+        row = k - 2
         gi, gf, gg, go = activated(k)
-        now = gf * cl[k] + gi * gg
+        now = gf * c0s[pl.ds(k * WD, WD), :] + gi * gg
         th = jnp.tanh(now)
         c1s[pl.ds(k * WD, WD), :] = now
-        if -1 <= row <= 4:
-            at = pl.ds((row + 1) * WD, WD)
+        if 0 <= row < RD:
+            at = pl.ds(row * WD, WD)
             for q, val in enumerate((gi, gf, gg, go, th)):
                 sv[q, at, :] = val
         h = (go * th).astype(BF).astype(F32)
         s2[pl.ds(EDGE + k * WD, WD), :] = h * row_mask(row)
     for b in range(KS):
-        hs2[b] = s2[pl.ds(EDGE + b - 1, 10 * WD), :].astype(BF)
-
-    gates_of(hs2, 1, 1, 8)
-
-    def backward(k, row, s, dh, gi, gf, gg, go, th, before, dg, own_at):
-        mask = row_mask(row)
-        pres = (
+        hs2[b] = s2[pl.ds(EDGE + b - 1, 8 * WD), :].astype(BF)
+
+    gates_of(hs2, 1, 2, 6)
+
+    def pre_grads(s, dh, gi, gf, gg, go, th, before):
+        return (
             s * gg * gi * (1.0 - gi),
             s * before * gf * (1.0 - gf),
             s * gi * (1.0 - gg * gg),
             dh * th * go * (1.0 - go),
         )
-        for q, pre in enumerate(pres):
-            cols = pl.ds(q * HC, HC)
-            masked = pre * mask
-            dg[pl.ds(k * WD, WD), cols] = masked.astype(BF)
-            if 0 <= row < RD:
-                dgo[pl.ds(own_at + row * WD, WD), cols] = (masked * own_mask).astype(BF)
-
-    for k in range(8):
-        row = k - 2
+
+    for k in range(6):
+        row = k - 1
         gi, gf, gg, go = activated(k)
         before = c1s[pl.ds((k + 1) * WD, WD), :]
         now = gf * before + gi * gg
         th = jnp.tanh(now)
+        dh = k1s[pl.ds(k * WD, WD), :]
+        s = dh * go * (1.0 - th * th)
         if 0 <= row < RD:
             hid_out[row] = (go * th)[8 : 8 + CD, :].astype(BF)
-        dh = kl[1, k].astype(F32)[8 : 8 + WD, :]
-        s = dh * go * (1.0 - th * th)
-        if -1 <= row <= 4:
-            dcs[pl.ds((row + 1) * WD, WD), :] = s * gf
-        backward(k, row, s, dh, gi, gf, gg, go, th, before, dg2, RD * WD)
+            dcs[pl.ds(row * WD, WD), :] = s * gf
+        mask = row_mask(row)
+        for q, pre in enumerate(pre_grads(s, dh, gi, gf, gg, go, th, before)):
+            cols = pl.ds(q * HC, HC)
+            dg2[pl.ds(k * WD, WD), cols] = (pre * mask).astype(BF)
+            if 0 <= row < RD:
+                dgo[pl.ds((RD + row) * WD, WD), cols] = (pre * own_mask).astype(BF)
 
     def adjoint(dg, count):
         size_m = count * WD
@@ -337,24 +383,30 @@
             preferred_element_type=F32,
         )
 
-    def gathered(k):
+    def gathered(k, count):
         total = None
         for tap in range(TAPS):
             a, b = divmod(tap, KS)
-            term = zs[pl.ds(EDGE + (k + 2 - a) * WD - (b - 1), WD), pl.ds(tap * HC, HC)]
+            row = k + 2 - a
+            if not 0 <= row < count:
+                continue
+            term = zs[pl.ds(EDGE + row * WD - (b - 1), WD), pl.ds(tap * HC, HC)]
             total = term if total is None else total + term
         return total
 
-    adjoint(dg2, 8)
-    for k in range(6):
-        row = k - 1
-        at = pl.ds(k * WD, WD)
+    adjoint(dg2, 6)
+    for row in range(RD):
+        at = pl.ds(row * WD, WD)
         gi, gf, gg, go, th = (sv[q, at, :] for q in range(5))
-        dh = gathered(k) + kl[0, k + 1].astype(F32)[8 : 8 + WD, :]
+        inner = gathered(row, 6)
+        cot = kown[0, row].astype(F32)
+        blank = jnp.zeros((8, HC), F32)
+        dh = inner + jnp.concatenate([blank, cot, blank], axis=0)
         s = dcs[at, :] + dh * go * (1.0 - th * th)
-        if 0 <= row < RD:
-            gc_out[row] = (s * gf)[8 : 8 + CD, :]
-        backward(k, row, s, dh, gi, gf, gg, go, th, cl[k + 2], dg1, 0)
+        gc_out[row] = (s * gf)[8 : 8 + CD, :]
+        before = c0s[pl.ds((row + 2) * WD, WD), :]
+        for q, pre in enumerate(pre_grads(s, dh, gi, gf, gg, go, th, before)):
+            dgo[at, pl.ds(q * HC, HC)] = (pre * own_mask).astype(BF)
 
     count = [0]
 
@@ -379,8 +431,8 @@
         for q in range(4 * p, 4 * p + 4):
             if q < TAPS:
                 a, b = divmod(q, KS)
-                one = hs1[b, pl.ds((3 + a) * WD, RD * WD), :]
-                two = hs2[b, pl.ds((2 + a) * WD, RD * WD), :]
+                one = hs1[b, pl.ds((2 + a) * WD, RD * WD), :]
+                two = hs2[b, pl.ds((1 + a) * WD, RD * WD), :]
             else:
                 a = q - TAPS
                 one = xb[0, pl.ds((3 + a) * WD, RD * WD), :]
@@ -403,10 +455,10 @@
         )
     sent += swaps
 
-    adjoint(dg1, 6)
-    for row in range(RD):
-        gh_out[row] = gathered(row)[8 : 8 + CD, :]
-
+    adjoint(dgo, RD)
+    zs[pl.ds(EDGE + RD * WD, EDGE), :] = wide
+    for k in range(RD + 2):
+        cb[k] = gathered(k - 2, RD)
     plans = [
         ("z", "y", "x", r1z, a2z, r2z, r3z),
         ("y", "z", "x", r1y, a2y, r2y, r3y),
@@ -469,6 +521,22 @@
             copies.append(copy)
         stage2.append(copies)
         sent += copies
+
+    late = []
+    for i, (dr, dc) in enumerate(SIDES):
+        rows_at = pl.ds(0, 1) if dr < 0 else (pl.ds(RD + 1, 1) if dr > 0 else pl.ds(1, RD))
+        cols_at = pl.ds(0, 8) if dc < 0 else (pl.ds(8 + CD, 8) if dc > 0 else pl.ds(8, CD))
+        copy = pltpu.make_async_remote_copy(
+            src_ref=cb.at[rows_at, cols_at, :],
+            dst_ref=slot_of(dr, dc, ud_c, lr_c, co_c),
+            send_sem=late_send.at[i],
+            recv_sem=late_recv.at[i],
+            device_id=neighbour(dr, dc),
+            device_id_type=MESH,
+        )
+        copy.start()
+        late.append(copy)
+    sent += late
 
     stage3 = []
     for p, (ax1, ax2, ax3, r1, a2, r2, r3) in enumerate(plans):
@@ -527,6 +595,18 @@
         stage5.append(copies)
         sent += copies
 
+    for copy in late:
+        copy.wait_recv()
+    for row in range(RD):
+        gh_out[row] = cb[row + 1, pl.ds(8, CD), :]
+    for dr, dc in SIDES:
+        inside = (r - dr >= 0) & (r - dr < n_rows) & (c - dc >= 0) & (c - dc < n_cols)
+        keep = jnp.where(inside, 1.0, 0.0).astype(F32)
+        rows_at = pl.ds(RD - 1, 1) if dr < 0 else (pl.ds(0, 1) if dr > 0 else pl.ds(0, RD))
+        cols_at = pl.ds(CD - 8, 8) if dc < 0 else (pl.ds(0, 8) if dc > 0 else pl.ds(0, CD))
+        terms = slot_of(dr, dc, ud_c, lr_c, co_c)[...] * keep
+        gh_out[rows_at, cols_at, :] = gh_out[rows_at, cols_at, :] + terms
+
     stage6 = []
     for p in range(PARTS):
         for copy in stage5[p]:
@@ -539,13 +619,7 @@
     for copy in stage6:
         copy.wait_recv()
 
-    for tap in range(TAPS):
-        a, b = divmod(tap, KS)
-        total_out[pl.ds(tap * 160, CI), :] = gs[
-            pl.ds(TAPS * HC + a * 128 + b * CI, CI), :
-        ]
-        total_out[pl.ds(tap * 160 + CI, HC), :] = gs[pl.ds(tap * HC, HC), :]
-    total_out[pl.ds(KIN, 16), :] = gs[pl.ds(BIAS_ROW, 16), :]
+    total_out[...] = gs[...]
 
     for copy in halos:
         copy.wait_send()
@@ -568,26 +642,37 @@
     ux = units(NX, NZ)
     vmem = pltpu.VMEM
     scratch = [
-        vmem((12, 64, HC), BF),
+        vmem((RD, CD, HC), BF),
         vmem((3, STEPS, RD, 1280), BF),
-        vmem((10, WD, HC), F32),
-        vmem((STEPS, 8, 64, HC), BF),
+        vmem((RD, CD, HC), F32),
+        vmem((STEPS, RD, CD, HC), BF),
         vmem((ROWS_W, GATES), BF),
+        vmem((2, 6 * CD, HC), BF),
+        vmem((2, 3 * RD * 8, HC), BF),
+        vmem((4, 6 * 8, HC), BF),
+        vmem((2, 6 * CD, HC), BF),
+        vmem((2, 3 * RD * 8, HC), BF),
+        vmem((4, 6 * 8, HC), BF),
         vmem((STEPS, 16, 1280), F32),
         vmem((STEPS, 12 * WD + 2 * EDGE, HC), F32),
         vmem((STEPS, 12 * WD, HC), BF),
-        vmem((12 * WD + 2 * EDGE, HC), F32),
         vmem((10 * WD + 2 * EDGE, HC), F32),
-        vmem((KS, 12 * WD, HC), BF),
+        vmem((8 * WD + 2 * EDGE, HC), F32),
         vmem((KS, 10 * WD, HC), BF),
-        vmem((10 * WD, GATES), F32),
-        vmem((5, 6 * WD, HC), F32),
-        vmem((10 * WD, HC), F32),
+        vmem((KS, 8 * WD, HC), BF),
+        vmem((8 * WD, GATES), F32),
+        vmem((5, RD * WD, HC), F32),
+        vmem((8 * WD, HC), F32),
+        vmem((8 * WD, HC), F32),
         vmem((6 * WD, HC), F32),
-        vmem((8 * WD, GATES), BF),
+        vmem((RD * WD, HC), F32),
         vmem((6 * WD, GATES), BF),
         vmem((2 * RD * WD, GATES), BF),
-        vmem((8 * WD + 2 * EDGE, TAPS * HC), F32),
+        vmem((6 * WD + 2 * EDGE, TAPS * HC), F32),
+        vmem((RD + 2, WD, HC), F32),
+        vmem((2, 1, CD, HC), F32),
+        vmem((2, RD, 8, HC), F32),
+        vmem((4, 1, 8, HC), F32),
         vmem((PARTS, PART, HALF), BF),
         vmem((PARTS, PART, HALF), F32),
         vmem((PARTS, PART, HALF), BF),
@@ -605,13 +690,15 @@
         vmem((NX,) + uy, BF),
         vmem((ny,) + ux, BF),
         vmem((ROWS_W, GATES), BF),
-        pltpu.SemaphoreType.DMA((8, 4)),
-        pltpu.SemaphoreType.DMA((8, 4)),
+        pltpu.SemaphoreType.DMA((8, 2)),
+        pltpu.SemaphoreType.DMA((8, 2)),
+        pltpu.SemaphoreType.DMA((8,)),
+        pltpu.SemaphoreType.DMA((8,)),
         pltpu.SemaphoreType.DMA((22,)),
         pltpu.SemaphoreType.DMA((stages(n_rows),)),
         pltpu.SemaphoreType.DMA((stages(n_rows),)),
     ]
-    anywhere = pl.BlockSpec(memory_space=pl.ANY)
+    in_hbm = pl.BlockSpec(memory_space=pltpu.HBM)
     in_vmem = pl.BlockSpec(memory_space=pltpu.VMEM)
     hidden, grad_hidden, grad_cell, total = pl.pallas_call(
         functools.partial(body, n_rows, n_cols),
@@ -619,9 +706,9 @@
             jax.ShapeDtypeStruct((RD, CD, HC), BF),
             jax.ShapeDtypeStruct((RD, CD, HC), F32),
             jax.ShapeDtypeStruct((RD, CD, HC), F32),
-            jax.ShapeDtypeStruct((KIN + 16, GATES), BF),
+            jax.ShapeDtypeStruct((ROWS_W, GATES), BF),
         ),
-        in_specs=[anywhere, anywhere, anywhere, anywhere, in_vmem, anywhere],
+        in_specs=[in_hbm, in_hbm, in_hbm, in_hbm, in_vmem, in_hbm],
         out_specs=(in_vmem, in_vmem, in_vmem, in_vmem),
         scratch_shapes=scratch,
         compiler_params=pltpu.CompilerParams(
@@ -629,9 +716,49 @@
         ),
     )(frames, hidden_start, cell_start, kernel, gate_bias.reshape(1, GATES), cotangent)
     scale = 1.0 / math.sqrt(STEPS * n_rows * RD * n_cols * CD)
-    kernel_grad = total[:KIN].astype(F32) * scale
-    bias_grad = total[KIN].astype(F32) * scale
-    return hidden, grad_hidden, grad_cell, kernel_grad, bias_grad
+    outs = pl.pallas_call(
+        functools.partial(finish, scale),
+        out_shape=(
+            jax.ShapeDtypeStruct((RD, CD, HC), BF),
+            jax.ShapeDtypeStruct((RD, CD, HC), F32),
+            jax.ShapeDtypeStruct((RD, CD, HC), F32),
+            jax.ShapeDtypeStruct((KIN, GATES), F32),
+            jax.ShapeDtypeStruct((1, GATES), F32),
+        ),
+        in_specs=[in_vmem] * 4,
+        out_specs=(in_hbm,) * 5,
+        scratch_shapes=[
+            vmem((KIN, GATES), F32),
+            vmem((1, GATES), F32),
+            pltpu.SemaphoreType.DMA((TAPS + 4,)),
+        ],
+        compiler_params=pltpu.CompilerParams(vmem_limit_bytes=16 * 1024 * 1024),
+    )(hidden, grad_hidden, grad_cell, total)
+    return outs[0], outs[1], outs[2], outs[3], outs[4].reshape(GATES)
+
+
+def finish(scale, hid, gh, gc, total, hid_out, gh_out, gc_out, kg_out, bg_out, kg, bg, sem):
+    copies = []
+
+    def put(src, dst):
+        copy = pltpu.make_async_copy(src, dst, sem.at[len(copies)])
+        copy.start()
+        copies.append(copy)
+
+    put(hid, hid_out)
+    put(gh, gh_out)
+    put(gc, gc_out)
+    for tap in range(TAPS):
+        a, b = divmod(tap, KS)
+        first = TAPS * HC + a * 128 + b * CI
+        at = tap * 160
+        kg[pl.ds(at, CI), :] = total[pl.ds(first, CI), :].astype(F32) * scale
+        kg[pl.ds(at + CI, HC), :] = total[pl.ds(tap * HC, HC), :].astype(F32) * scale
+        put(kg.at[pl.ds(at, 160), :], kg_out.at[pl.ds(at, 160), :])
+    bg[...] = total[pl.ds(BIAS_ROW, 16), :].astype(F32)[:1, :] * scale
+    put(bg, bg_out)
+    for copy in copies:
+        copy.wait()
 
 
 def stages(n_rows):

time: 79.7 us -> 70.4 us (0.88)
  Pallas kernels: 69 us -> 64.2 us
  other arithmetic: 2.62 us -> 0 us
  local copies, waits for them, and re-layouts: 7.07 us -> 5.2 us
    pallas_call x1, Pallas kernels: 69 us -> 62.4 us  [shards(): pl.pallas_call(functools.partial(body, n_rows, n_cols), out_shape=(jax.Sh...]
    mul x2 -> x0, other arithmetic: 2.62 us -> none  [the longest x1 2.04 us: shards(): kernel_grad = total[:KIN].astype(F32) * scale]
    unnamed x15 -> x12, local copies, waits for them, and re-layouts: 7.07 us -> 5.2 us
    pallas_call x0 -> x1, Pallas kernels: none -> 1.76 us  [shards(): pl.pallas_call(functools.partial(finish, scale), out_shape=(jax.ShapeDtyp...]
where the time goes in v2:
time: 70.4 us; the launch traced here: 70.1 us
  Pallas kernels  64.2 us (91%)
  local copies, waits for them, and re-layouts  5.2 us (7%)
    pallas_call x1, Pallas kernels, shards(): pl.pallas_call(functools.partial(body, n_rows, n_cols), out_shape=(jax.Sh...  62.4 us
    unnamed x12, local copies, waits for them, and re-layouts  5.2 us
    pallas_call x1, Pallas kernels, shards(): pl.pallas_call(functools.partial(finish, scale), out_shape=(jax.ShapeDtyp...  1.76 us

profile of v2, /device:TPU:1, one launch (start us, length us, event | category | flops | bytes accessed | tf_op | source)
XLA Modules:
  0.0 70.1 jit_solution(14005378223601102770)
XLA Ops:
  0.6 0.0 copy-start
  0.6 1.4 %copy-done = bf16[1440,512]{1,0:T(8,128)(2,1)S(1)} copy-done((bf16[1440,512]{1,0:T(8,128)(2,1)S(1)}, bf16[1440,512]{1,0:T(8,128)(2,1)}, u32[]{:S(2)}) %copy-start) | copy-done | bytes 1474584
  2.0 0.0 copy-start.1
  2.0 0.8 %copy-done.1 = f32[4,32,128]{2,1,0:T(8,128)S(1)} copy-done((f32[4,32,128]{2,1,0:T(8,128)S(1)}, f32[4,32,128]{2,1,0:T(8,128)}, u32[]{:S(2)}) %copy-start.1) | copy-done | bytes 65560
  2.8 0.0 copy-start.2
  2.8 0.8 %copy-done.2 = bf16[2,4,32,128]{3,2,1,0:T(8,128)(2,1)S(1)} copy-done((bf16[2,4,32,128]{3,2,1,0:T(8,128)(2,1)S(1)}, bf16[2,4,32,128]{3,2,1,0:T(8,128)(2,1)}, u32[]{:S(2)}) %copy-start.2) | copy-done | bytes 65560
  3.7 0.0 copy-start.3
  3.7 0.8 %copy-done.3 = bf16[4,32,128]{2,1,0:T(8,128)(2,1)S(1)} copy-done((bf16[4,32,128]{2,1,0:T(8,128)(2,1)S(1)}, bf16[4,32,128]{2,1,0:T(8,128)(2,1)}, u32[]{:S(2)}) %copy-start.3) | copy-done | bytes 32792
  4.4 0.0 copy-start.4
  4.4 0.7 %copy-done.4 = bf16[2,4,1024]{2,1,0:T(4,128)(2,1)S(1)} copy-done((bf16[2,4,1024]{2,1,0:T(4,128)(2,1)S(1)}, bf16[2,4,1024]{2,1,0:T(4,128)(2,1)}, u32[]{:S(2)}) %copy-start.4) | copy-done | bytes 16408
  5.2 0.0 copy-start.5
  5.2 0.7 copy-done.5
  5.8 62.4 %shard_map.101 = (bf16[4,32,128]{2,1,0:T(8,128)(2,1)S(1)}, f32[4,32,128]{2,1,0:T(8,128)S(1)}, f32[4,32,128]{2,1,0:T(8,128)S(1)}, bf16[1536,512]{1,0:T(8,128)(2,1)S(1)}) custom-call(bf16[2,4,1024]{2,1,0:T(4,128)(2,1)S(1)} %copy-done.4, bf16[4,32,128]{2,1,0:T(8,128)(2,1)S(1)} %copy-done.3, f32[4,32,128]{2,1,0:T(8,128)S(1)} %copy-done.1, ...), custom_call_target="tpu_custom_call" | custom-call | tf_op jit(solution)/shard_map/pallas_call | solution.py:703
  68.3 1.8 %shard_map.102 = (bf16[4,32,128]{2,1,0:T(8,128)(2,1)}, f32[4,32,128]{2,1,0:T(8,128)}, f32[4,32,128]{2,1,0:T(8,128)}, f32[1440,512]{1,0:T(8,128)}, f32[1,512]{1,0:T(1,128)}) custom-call(bf16[4,32,128]{2,1,0:T(8,128)(2,1)S(1)} %get-tuple-element.14.hid, f32[4,32,128]{2,1,0:T(8,128)S(1)} %get-tuple-element.15.gh, f32[4,32,128]{2,1,0:T(8,128)S(1)} %get-tuple-element.16.gc, ...), custom_call_target="tpu_custom_call" | custom-call | tf_op jit(solution)/shard_map/pallas_call | solution.py:719
Async XLA Ops:
  0.6 1.4 %copy-start = (bf16[1440,512]{1,0:T(8,128)(2,1)S(1)}, bf16[1440,512]{1,0:T(8,128)(2,1)}, u32[]{:S(2)}) copy-start(bf16[1440,512]{1,0:T(8,128)(2,1)} %kernel_ref.1) | copy-start | bytes 4423684
  2.0 0.8 %copy-start.1 = (f32[4,32,128]{2,1,0:T(8,128)S(1)}, f32[4,32,128]{2,1,0:T(8,128)}, u32[]{:S(2)}) copy-start(f32[4,32,128]{2,1,0:T(8,128)} %cell_ref.1) | copy-start | bytes 196612
  2.8 0.8 %copy-start.2 = (bf16[2,4,32,128]{3,2,1,0:T(8,128)(2,1)S(1)}, bf16[2,4,32,128]{3,2,1,0:T(8,128)(2,1)}, u32[]{:S(2)}) copy-start(bf16[2,4,32,128]{3,2,1,0:T(8,128)(2,1)} %cot_ref.1) | copy-start | bytes 196612
  3.7 0.8 %copy-start.3 = (bf16[4,32,128]{2,1,0:T(8,128)(2,1)S(1)}, bf16[4,32,128]{2,1,0:T(8,128)(2,1)}, u32[]{:S(2)}) copy-start(bf16[4,32,128]{2,1,0:T(8,128)(2,1)} %hidden_ref.1) | copy-start | bytes 98308
  4.4 0.7 %copy-start.4 = (bf16[2,4,1024]{2,1,0:T(4,128)(2,1)S(1)}, bf16[2,4,1024]{2,1,0:T(4,128)(2,1)}, u32[]{:S(2)}) copy-start(bf16[2,4,1024]{2,1,0:T(4,128)(2,1)} %frames_ref.1) | copy-start | bytes 49156
  5.2 0.7 copy-start.5

commit v3 on v2

--- a/solution.py
+++ b/solution.py
@@ -57,10 +57,14 @@
     kernel_ref,
     bias_ref,
     cot_ref,
+    hid_hbm,
+    gh_hbm,
+    gc_hbm,
+    total_hbm,
     hid_out,
     gh_out,
     gc_out,
-    total_out,
+    bias_in,
     hown,
     fl,
     cown,
@@ -114,6 +118,7 @@
     late_send,
     late_recv,
     loc_sem,
+    out_sem,
     st_send,
     st_recv,
 ):
@@ -155,6 +160,7 @@
     fetch(cell_ref, cown)
     fetch(cot_ref, kown)
     fetch(frames_ref, fl.at[1, :, :, pl.ds(128, CD * CI)])
+    fetch(bias_ref, bias_in)
     for tap in range(TAPS):
         a, b = divmod(tap, KS)
         fetch(kernel_ref.at[pl.ds(tap * 160 + CI, HC), :], wp.at[pl.ds(tap * HC, HC), :])
@@ -308,7 +314,7 @@
             )
             xb[t, pl.ds(row * WD, WD), :] = joined.astype(BF)
 
-    bias = bias_ref[...]
+    bias = bias_in[...]
 
     def gates_of(hs, t, first, count):
         size_m = count * WD
@@ -408,6 +414,16 @@
         for q, pre in enumerate(pre_grads(s, dh, gi, gf, gg, go, th, before)):
             dgo[at, pl.ds(q * HC, HC)] = (pre * own_mask).astype(BF)
 
+    written = []
+
+    def write(src, dst):
+        copy = pltpu.make_async_copy(src, dst, out_sem.at[len(written)])
+        copy.start()
+        written.append(copy)
+
+    write(hid_out, hid_hbm)
+    write(gc_out, gc_hbm)
+
     count = [0]
 
     def copy_to(src, dst, who):
@@ -441,24 +457,20 @@
         return jnp.concatenate(blocks, axis=1)
 
     swaps = []
+    dims = (((0,), (0,)), ((), ()))
     for p in range(PARTS):
-        lhs = weight_blocks(p)
-        dims = (((0,), (0,)), ((), ()))
         a0[p] = lax.dot_general(
-            lhs, dgo[:, pl.ds(other_at, HALF)], dims, preferred_element_type=F32
+            weight_blocks(p), dgo[:, pl.ds(other_at, HALF)], dims, preferred_element_type=F32
         ).astype(BF)
         copy = copy_to(a0.at[p], r0.at[p], sibling)
         copy.start()
         swaps.append(copy)
+    for p in range(PARTS):
         o0[p] = lax.dot_general(
-            lhs, dgo[:, pl.ds(mine_at, HALF)], dims, preferred_element_type=F32
+            weight_blocks(p), dgo[:, pl.ds(mine_at, HALF)], dims, preferred_element_type=F32
         )
     sent += swaps
 
-    adjoint(dgo, RD)
-    zs[pl.ds(EDGE + RD * WD, EDGE), :] = wide
-    for k in range(RD + 2):
-        cb[k] = gathered(k - 2, RD)
     plans = [
         ("z", "y", "x", r1z, a2z, r2z, r3z),
         ("y", "z", "x", r1y, a2y, r2y, r3y),
@@ -501,6 +513,10 @@
         stage1.append(copies)
         sent += copies
 
+    adjoint(dgo, RD)
+    zs[pl.ds(EDGE + RD * WD, EDGE), :] = wide
+    for k in range(RD + 2):
+        cb[k] = gathered(k - 2, RD)
     stage2 = []
     for p, (ax1, ax2, ax3, r1, a2, r2, r3) in enumerate(plans):
         n1, n2, n3, rows1, unit, unit_at = state[p]
@@ -607,20 +623,28 @@
         terms = slot_of(dr, dc, ud_c, lr_c, co_c)[...] * keep
         gh_out[rows_at, cols_at, :] = gh_out[rows_at, cols_at, :] + terms
 
+    write(gh_out, gh_hbm)
+
     stage6 = []
     for p in range(PARTS):
         for copy in stage5[p]:
             copy.wait_recv()
-        slot = gs.at[pl.ds(p * PART, PART), pl.ds(mine_at, HALF)]
+        rows_at = pl.ds(p * PART, PART)
+        slot = gs.at[rows_at, pl.ds(mine_at, HALF)]
         copy = copy_to(slot, slot, sibling)
         copy.start()
         stage6.append(copy)
+        write(slot, total_hbm.at[rows_at, pl.ds(mine_at, HALF)])
     sent += stage6
-    for copy in stage6:
+    for p, copy in enumerate(stage6):
         copy.wait_recv()
-
-    total_out[...] = gs[...]
-
+        rows_at = pl.ds(p * PART, PART)
+        write(
+            gs.at[rows_at, pl.ds(other_at, HALF)], total_hbm.at[rows_at, pl.ds(other_at, HALF)]
+        )
+
+    for copy in written:
+        copy.wait()
     for copy in halos:
         copy.wait_send()
     for copy in sent:
@@ -642,6 +666,10 @@
     ux = units(NX, NZ)
     vmem = pltpu.VMEM
     scratch = [
+        vmem((RD, CD, HC), BF),
+        vmem((RD, CD, HC), F32),
+        vmem((RD, CD, HC), F32),
+        vmem((1, GATES), F32),
         vmem((RD, CD, HC), BF),
         vmem((3, STEPS, RD, 1280), BF),
         vmem((RD, CD, HC), F32),
@@ -694,12 +722,12 @@
         pltpu.SemaphoreType.DMA((8, 2)),
         pltpu.SemaphoreType.DMA((8,)),
         pltpu.SemaphoreType.DMA((8,)),
-        pltpu.SemaphoreType.DMA((22,)),
+        pltpu.SemaphoreType.DMA((5 + 2 * TAPS,)),
+        pltpu.SemaphoreType.DMA((3 + 2 * PARTS,)),
         pltpu.SemaphoreType.DMA((stages(n_rows),)),
         pltpu.SemaphoreType.DMA((stages(n_rows),)),
     ]
     in_hbm = pl.BlockSpec(memory_space=pltpu.HBM)
-    in_vmem = pl.BlockSpec(memory_space=pltpu.VMEM)
     hidden, grad_hidden, grad_cell, total = pl.pallas_call(
         functools.partial(body, n_rows, n_cols),
         out_shape=(
@@ -708,11 +736,11 @@
             jax.ShapeDtypeStruct((RD, CD, HC), F32),
             jax.ShapeDtypeStruct((ROWS_W, GATES), BF),
         ),
-        in_specs=[in_hbm, in_hbm, in_hbm, in_hbm, in_vmem, in_hbm],
-        out_specs=(in_vmem, in_vmem, in_vmem, in_vmem),
+        in_specs=[in_hbm] * 6,
+        out_specs=(in_hbm,) * 4,
         scratch_shapes=scratch,
         compiler_params=pltpu.CompilerParams(
-            collective_id=0, has_side_effects=True, vmem_limit_bytes=48 * 1024 * 1024
+            collective_id=0, has_side_effects=True, vmem_limit_bytes=63 * 1024 * 1024
         ),
     )(frames, hidden_start, cell_start, kernel, gate_bias.reshape(1, GATES), cotangent)
     scale = 1.0 / math.sqrt(STEPS * n_rows * RD * n_cols * CD)
@@ -725,19 +753,23 @@
             jax.ShapeDtypeStruct((KIN, GATES), F32),
             jax.ShapeDtypeStruct((1, GATES), F32),
         ),
-        in_specs=[in_vmem] * 4,
+        in_specs=[in_hbm] * 4,
         out_specs=(in_hbm,) * 5,
         scratch_shapes=[
+            vmem((ROWS_W, GATES), BF),
             vmem((KIN, GATES), F32),
             vmem((1, GATES), F32),
+            pltpu.SemaphoreType.DMA((1 + KS,)),
             pltpu.SemaphoreType.DMA((TAPS + 4,)),
         ],
-        compiler_params=pltpu.CompilerParams(vmem_limit_bytes=16 * 1024 * 1024),
+        compiler_params=pltpu.CompilerParams(vmem_limit_bytes=63 * 1024 * 1024),
     )(hidden, grad_hidden, grad_cell, total)
     return outs[0], outs[1], outs[2], outs[3], outs[4].reshape(GATES)
 
 
-def finish(scale, hid, gh, gc, total, hid_out, gh_out, gc_out, kg_out, bg_out, kg, bg, sem):
+def finish(
+    scale, hid, gh, gc, total_hbm, hid_out, gh_out, gc_out, kg_out, bg_out, total, kg, bg, in_sem, sem
+):
     copies = []
 
     def put(src, dst):
@@ -745,11 +777,21 @@
         copy.start()
         copies.append(copy)
 
+    fetched = []
+    step = KS * HC
+    for i in range(1 + KS):
+        at = pl.ds(TAPS * HC if i == 0 else (i - 1) * step, step)
+        copy = pltpu.make_async_copy(total_hbm.at[at, :], total.at[at, :], in_sem.at[i])
+        copy.start()
+        fetched.append(copy)
     put(hid, hid_out)
     put(gh, gh_out)
     put(gc, gc_out)
+    fetched[0].wait()
     for tap in range(TAPS):
         a, b = divmod(tap, KS)
+        if b == 0:
+            fetched[1 + a].wait()
         first = TAPS * HC + a * 128 + b * CI
         at = tap * 160
         kg[pl.ds(at, CI), :] = total[pl.ds(first, CI), :].astype(F32) * scale

time: 70.4 us -> 70.5 us (level)
  Pallas kernels: 64.2 us -> 69.7 us
  local copies, waits for them, and re-layouts: 5.2 us -> 0 us
    unnamed x12 -> x0, local copies, waits for them, and re-layouts: 5.2 us -> none
    pallas_call x1, Pallas kernels: 1.76 us -> 6.24 us  [shards(): pl.pallas_call(functools.partial(finish, scale), out_shape=(jax.ShapeDtyp...]
    pallas_call x1, Pallas kernels: 62.4 us -> 63.5 us  [shards(): pl.pallas_call(functools.partial(body, n_rows, n_cols), out_shape=(jax.Sh...]
where the time goes in v3:
time: 70.5 us; the launch traced here: 70.4 us
  Pallas kernels  69.7 us (99%)
    pallas_call x1, Pallas kernels, shards(): pl.pallas_call(functools.partial(body, n_rows, n_cols), out_shape=(jax.Sh...  63.5 us
    pallas_call x1, Pallas kernels, shards(): pl.pallas_call(functools.partial(finish, scale), out_shape=(jax.ShapeDtyp...  6.24 us

profile of v3, /device:TPU:1, one launch (start us, length us, event | category | flops | bytes accessed | tf_op | source)
XLA Modules:
  0.0 70.4 jit_solution(9401671387867748734)
XLA Ops:
  0.6 63.5 %shard_map.101 = (bf16[4,32,128]{2,1,0:T(8,128)(2,1)}, f32[4,32,128]{2,1,0:T(8,128)}, f32[4,32,128]{2,1,0:T(8,128)}, bf16[1536,512]{1,0:T(8,128)(2,1)}) custom-call(bf16[2,4,1024]{2,1,0:T(4,128)(2,1)} %frames_ref.1, bf16[4,32,128]{2,1,0:T(8,128)(2,1)} %hidden_ref.1, f32[4,32,128]{2,1,0:T(8,128)} %cell_ref.1, bf16[1440,512]{1,0:T(8,128)(2,1)} %kernel_ref.1, ...), custom_call_target="tpu_custom_call" | custom-call | tf_op jit(solution)/shard_map/pallas_call | solution.py:731
  64.1 6.2 %shard_map.102 = (bf16[4,32,128]{2,1,0:T(8,128)(2,1)}, f32[4,32,128]{2,1,0:T(8,128)}, f32[4,32,128]{2,1,0:T(8,128)}, f32[1440,512]{1,0:T(8,128)}, f32[1,512]{1,0:T(1,128)}) custom-call(bf16[4,32,128]{2,1,0:T(8,128)(2,1)} %get-tuple-element.14.hid, f32[4,32,128]{2,1,0:T(8,128)} %get-tuple-element.15.gh, f32[4,32,128]{2,1,0:T(8,128)} %get-tuple-element.16.gc, ...), custom_call_target="tpu_custom_call" | custom-call | tf_op jit(solution)/shard_map/pallas_call | solution.py:747

commit v4 on v3

--- a/solution.py
+++ b/solution.py
@@ -30,9 +30,11 @@
 EDGE = 8
 ROWS_W = 1536
 PARTS = 3
-PART = ROWS_W // PARTS
 HALF = GATES // 2
-BIAS_ROW = TAPS * HC + 3 * CI
+FRAME_ROWS = ((0, 112), (112, 96), (208, 96))
+AREAS = ((0, 384), (768, 384), (1536, 704))
+LINES = 2944
+BIAS_ROW = 384 + 3 * CI
 SIDES = [(dr, dc) for dr in (-1, 0, 1) for dc in (-1, 0, 1) if (dr, dc) != (0, 0)]
 
 
@@ -112,6 +114,9 @@
     r3z,
     r3y,
     r3x,
+    g4z,
+    g4y,
+    g4x,
     gs,
     halo_send,
     halo_recv,
@@ -235,6 +240,8 @@
     zs[pl.ds(0, EDGE), :] = wide
     zs[pl.ds(EDGE + 6 * WD, EDGE), :] = wide
     fs[...] = jnp.zeros_like(fs)
+    for spare in (a2z, a2y, a2x):
+        spare[...] = jnp.zeros_like(spare)
 
     at_col = lax.broadcasted_iota(jnp.int32, (WD, HC), 0) - 8
     in_raster = (at_col + c * CD >= 0) & (at_col + c * CD < n_cols * CD)
@@ -444,7 +451,7 @@
 
     def weight_blocks(p):
         blocks = []
-        for q in range(4 * p, 4 * p + 4):
+        for q in range(KS * p, KS * p + (KS if p < 2 else 2 * KS)):
             if q < TAPS:
                 a, b = divmod(q, KS)
                 one = hs1[b, pl.ds((2 + a) * WD, RD * WD), :]
@@ -456,58 +463,52 @@
             blocks.append(jnp.concatenate([one, two], axis=0))
         return jnp.concatenate(blocks, axis=1)
 
+    def weight_grad(p, cols_at, out):
+        val = lax.dot_general(
+            weight_blocks(p),
+            dgo[:, pl.ds(cols_at, HALF)],
+            (((0,), (0,)), ((), ())),
+            preferred_element_type=F32,
+        ).astype(out.dtype)
+        base, lines = AREAS[p]
+        for panel in range(2):
+            cut = val[:, panel * 128 : (panel + 1) * 128]
+            at = base + panel * lines
+            out[pl.ds(at, KS * HC), :] = cut[: KS * HC, :]
+            if p == 2:
+                for a, (first, size_a) in enumerate(FRAME_ROWS):
+                    start = (KS + a) * HC
+                    out[pl.ds(at + KS * HC + first, size_a), :] = cut[start : start + size_a, :]
+                out[pl.ds(at + lines - 16, 16), :] = jnp.zeros((16, 128), out.dtype)
+
     swaps = []
-    dims = (((0,), (0,)), ((), ()))
-    for p in range(PARTS):
-        a0[p] = lax.dot_general(
-            weight_blocks(p), dgo[:, pl.ds(other_at, HALF)], dims, preferred_element_type=F32
-        ).astype(BF)
-        copy = copy_to(a0.at[p], r0.at[p], sibling)
+    for p, (base, lines) in enumerate(AREAS):
+        weight_grad(p, other_at, a0)
+        area = pl.ds(base, 2 * lines)
+        copy = copy_to(a0.at[area, :], r0.at[area, :], sibling)
         copy.start()
         swaps.append(copy)
     for p in range(PARTS):
-        o0[p] = lax.dot_general(
-            weight_blocks(p), dgo[:, pl.ds(mine_at, HALF)], dims, preferred_element_type=F32
-        )
+        weight_grad(p, mine_at, o0)
     sent += swaps
 
     plans = [
-        ("z", "y", "x", r1z, a2z, r2z, r3z),
-        ("y", "z", "x", r1y, a2y, r2y, r3y),
-        ("x", "z", "y", r1x, a2x, r2x, r3x),
+        ("z", "y", "x", r1z, a2z, r2z, r3z, g4z),
+        ("y", "z", "x", r1y, a2y, r2y, r3y, g4y),
+        ("x", "z", "y", r1x, a2x, r2x, r3x, g4x),
     ]
-    state = []
-    for p, (ax1, ax2, ax3, r1, a2, r2, r3) in enumerate(plans):
-        n1, n2, n3 = size[ax1], size[ax2], size[ax3]
-        rows1 = PART // n1
-        rows2 = rows1 // n2
-        if rows2 >= 16:
-            unit = (rows2, HALF)
-        else:
-            unit = (16, HALF * rows2 // 16)
-        across = HALF // unit[1]
-
-        def unit_at(u, unit=unit, across=across):
-            return (
-                pl.multiple_of((u // across) * unit[0], 16),
-                pl.multiple_of(lax.rem(u, across) * unit[1], 128),
-            )
-
-        state.append((n1, n2, n3, rows1, unit, unit_at))
 
     stage1 = []
-    for p, (ax1, ax2, ax3, r1, a2, r2, r3) in enumerate(plans):
-        n1, n2, n3, rows1, unit, unit_at = state[p]
+    for p, (ax1, ax2, ax3, r1, a2, r2, r3, g4) in enumerate(plans):
+        base, lines = AREAS[p]
+        n1, chunk = size[ax1], r1.shape[1]
         swaps[p].wait_recv()
-        a1[p] = (o0[p] + r0[p].astype(F32)).astype(BF)
+        area = pl.ds(base, 2 * lines)
+        a1[area, :] = (o0[area, :] + r0[area, :].astype(F32)).astype(BF)
         copies = []
         for d in range(1, n1):
-            to = lax.rem(mine[ax1] + d, n1)
-            copy = copy_to(
-                a1.at[p, pl.ds(pl.multiple_of(to * rows1, 16), rows1), :],
-                r1.at[d - 1],
-                peer(ax1, d),
-            )
+            to = pl.multiple_of(base + lax.rem(mine[ax1] + d, n1) * chunk, 16)
+            copy = copy_to(a1.at[pl.ds(to, chunk), :], r1.at[d - 1], peer(ax1, d))
             copy.start()
             copies.append(copy)
         stage1.append(copies)
@@ -518,21 +519,21 @@
     for k in range(RD + 2):
         cb[k] = gathered(k - 2, RD)
     stage2 = []
-    for p, (ax1, ax2, ax3, r1, a2, r2, r3) in enumerate(plans):
-        n1, n2, n3, rows1, unit, unit_at = state[p]
+    for p, (ax1, ax2, ax3, r1, a2, r2, r3, g4) in enumerate(plans):
+        base, lines = AREAS[p]
+        n1, chunk = size[ax1], r1.shape[1]
+        n2, unit = size[ax2], r2.shape[1]
         for copy in stage1[p]:
             copy.wait_recv()
-        at = pl.ds(pl.multiple_of(mine[ax1] * rows1, 16), rows1)
-        total = a1[p, at, :].astype(F32)
+        at = pl.multiple_of(base + mine[ax1] * chunk, 16)
+        total = a1[pl.ds(at, chunk), :].astype(F32)
         for d in range(1, n1):
             total = total + r1[d - 1].astype(F32)
-        a2[...] = total.astype(BF)
+        a2[pl.ds(0, chunk), :] = total.astype(BF)
         copies = []
         for d in range(1, n2):
-            ur, uc = unit_at(lax.rem(mine[ax2] + d, n2))
-            copy = copy_to(
-                a2.at[pl.ds(ur, unit[0]), pl.ds(uc, unit[1])], r2.at[d - 1], peer(ax2, d)
-            )
+            to = pl.multiple_of(lax.rem(mine[ax2] + d, n2) * unit, 16)
+            copy = copy_to(a2.at[pl.ds(to, unit), :], r2.at[d - 1], peer(ax2, d))
             copy.start()
             copies.append(copy)
         stage2.append(copies)
@@ -555,12 +556,11 @@
     sent += late
 
     stage3 = []
-    for p, (ax1, ax2, ax3, r1, a2, r2, r3) in enumerate(plans):
-        n1, n2, n3, rows1, unit, unit_at = state[p]
+    for p, (ax1, ax2, ax3, r1, a2, r2, r3, g4) in enumerate(plans):
+        n2, n3, unit = size[ax2], size[ax3], r2.shape[1]
         for copy in stage2[p]:
             copy.wait_recv()
-        ur, uc = unit_at(mine[ax2])
-        total = a2[pl.ds(ur, unit[0]), pl.ds(uc, unit[1])].astype(F32)
+        total = a2[pl.ds(pl.multiple_of(mine[ax2] * unit, 16), unit), :].astype(F32)
         for d in range(1, n2):
             total = total + r2[d - 1].astype(F32)
         r3[mine[ax3]] = total.astype(BF)
@@ -573,18 +573,14 @@
         sent += copies
 
     stage4 = []
-    for p, (ax1, ax2, ax3, r1, a2, r2, r3) in enumerate(plans):
-        n1, n2, n3, rows1, unit, unit_at = state[p]
+    for p, (ax1, ax2, ax3, r1, a2, r2, r3, g4) in enumerate(plans):
+        n2, n3, unit = size[ax2], size[ax3], r2.shape[1]
         for copy in stage3[p]:
             copy.wait_recv()
         total = r3[0].astype(F32)
         for d in range(1, n3):
             total = total + r3[d].astype(F32)
-        ur, uc = unit_at(mine[ax2])
-        slot = gs.at[
-            pl.ds(pl.multiple_of(p * PART + mine[ax1] * rows1 + ur, 16), unit[0]),
-            pl.ds(pl.multiple_of(mine_at + uc, 128), unit[1]),
-        ]
+        slot = g4.at[pl.ds(pl.multiple_of(mine[ax2] * unit, 16), unit), :]
         slot[...] = total.astype(BF)
         copies = []
         for d in range(1, n2):
@@ -595,19 +591,18 @@
         sent += copies
 
     stage5 = []
-    for p, (ax1, ax2, ax3, r1, a2, r2, r3) in enumerate(plans):
-        n1, n2, n3, rows1, unit, unit_at = state[p]
+    for p, (ax1, ax2, ax3, r1, a2, r2, r3, g4) in enumerate(plans):
+        base, lines = AREAS[p]
+        n1, chunk = size[ax1], r1.shape[1]
         for copy in stage4[p]:
             copy.wait_recv()
-        slot = gs.at[
-            pl.ds(pl.multiple_of(p * PART + mine[ax1] * rows1, 16), rows1),
-            pl.ds(mine_at, HALF),
-        ]
+        at = pl.ds(pl.multiple_of(base + mine[ax1] * chunk, 16), chunk)
         copies = []
         for d in range(1, n1):
-            copy = copy_to(slot, slot, peer(ax1, d))
+            copy = copy_to(g4.at[pl.ds(0, chunk), :], gs.at[core, at, :], peer(ax1, d))
             copy.start()
             copies.append(copy)
+        gs[core, at, :] = g4[pl.ds(0, chunk), :]
         stage5.append(copies)
         sent += copies
 
@@ -626,22 +621,20 @@
     write(gh_out, gh_hbm)
 
     stage6 = []
-    for p in range(PARTS):
+    for p, (base, lines) in enumerate(AREAS):
         for copy in stage5[p]:
             copy.wait_recv()
-        rows_at = pl.ds(p * PART, PART)
-        slot = gs.at[rows_at, pl.ds(mine_at, HALF)]
+        slot = gs.at[core, pl.ds(base, 2 * lines), :]
         copy = copy_to(slot, slot, sibling)
         copy.start()
         stage6.append(copy)
-        write(slot, total_hbm.at[rows_at, pl.ds(mine_at, HALF)])
+        write(slot, total_hbm.at[core, pl.ds(base, 2 * lines), :])
     sent += stage6
     for p, copy in enumerate(stage6):
+        base, lines = AREAS[p]
         copy.wait_recv()
-        rows_at = pl.ds(p * PART, PART)
-        write(
-            gs.at[rows_at, pl.ds(other_at, HALF)], total_hbm.at[rows_at, pl.ds(other_at, HALF)]
-        )
+        area = pl.ds(base, 2 * lines)
+        write(gs.at[1 - core, area, :], total_hbm.at[1 - core, area, :])
 
     for copy in written:
         copy.wait()
@@ -651,19 +644,16 @@
         copy.wait_send()
 
 
-def units(n1, n2):
-    rows1 = PART // n1
-    rows2 = rows1 // n2
-    return (rows2, HALF) if rows2 >= 16 else (16, HALF * rows2 // 16)
+def sizes(p, n1, n2):
+    chunk = 2 * AREAS[p][1] // n1
+    return chunk, -(-chunk // (16 * n2)) * 16
 
 
 def shards(frames, hidden_start, cell_start, kernel, gate_bias, cotangent):
     n_rows = lax.axis_size("rows")
     n_cols = lax.axis_size("cols")
     ny = (n_rows // NX) * NYL
-    uz = units(NZ, ny)
-    uy = units(ny, NZ)
-    ux = units(NX, NZ)
+    (cz, uz), (cy, uy), (cx, ux) = sizes(0, NZ, ny), sizes(1, ny, NZ), sizes(2, NX, NZ)
     vmem = pltpu.VMEM
     scratch = [
         vmem((RD, CD, HC), BF),
@@ -701,23 +691,26 @@
         vmem((2, 1, CD, HC), F32),
         vmem((2, RD, 8, HC), F32),
         vmem((4, 1, 8, HC), F32),
-        vmem((PARTS, PART, HALF), BF),
-        vmem((PARTS, PART, HALF), F32),
-        vmem((PARTS, PART, HALF), BF),
-        vmem((PARTS, PART, HALF), BF),
-        vmem((NZ - 1, PART // NZ, HALF), BF),
-        vmem((ny - 1, PART // ny, HALF), BF),
-        vmem((NX - 1, PART // NX, HALF), BF),
-        vmem((PART // NZ, HALF), BF),
-        vmem((PART // ny, HALF), BF),
-        vmem((PART // NX, HALF), BF),
-        vmem((ny - 1,) + uz, BF),
-        vmem((NZ - 1,) + uy, BF),
-        vmem((NZ - 1,) + ux, BF),
-        vmem((NX,) + uz, BF),
-        vmem((NX,) + uy, BF),
-        vmem((ny,) + ux, BF),
-        vmem((ROWS_W, GATES), BF),
+        vmem((LINES, 128), BF),
+        vmem((LINES, 128), F32),
+        vmem((LINES, 128), BF),
+        vmem((LINES, 128), BF),
+        vmem((NZ - 1, cz, 128), BF),
+        vmem((ny - 1, cy, 128), BF),
+        vmem((NX - 1, cx, 128), BF),
+        vmem((ny * uz, 128), BF),
+        vmem((NZ * uy, 128), BF),
+        vmem((NZ * ux, 128), BF),
+        vmem((ny - 1, uz, 128), BF),
+        vmem((NZ - 1, uy, 128), BF),
+        vmem((NZ - 1, ux, 128), BF),
+        vmem((NX, uz, 128), BF),
+        vmem((NX, uy, 128), BF),
+        vmem((ny, ux, 128), BF),
+        vmem((ny * uz, 128), BF),
+        vmem((NZ * uy, 128), BF),
+        vmem((NZ * ux, 128), BF),
+        vmem((2, LINES, 128), BF),
         pltpu.SemaphoreType.DMA((8, 2)),
         pltpu.SemaphoreType.DMA((8, 2)),
         pltpu.SemaphoreType.DMA((8,)),
@@ -734,7 +727,7 @@
             jax.ShapeDtypeStruct((RD, CD, HC), BF),
             jax.ShapeDtypeStruct((RD, CD, HC), F32),
             jax.ShapeDtypeStruct((RD, CD, HC), F32),
-            jax.ShapeDtypeStruct((ROWS_W, GATES), BF),
+            jax.ShapeDtypeStruct((2, LINES, 128), BF),
         ),
         in_specs=[in_hbm] * 6,
         out_specs=(in_hbm,) * 4,
@@ -756,10 +749,13 @@
         in_specs=[in_hbm] * 4,
         out_specs=(in_hbm,) * 5,
         scratch_shapes=[
-            vmem((ROWS_W, GATES), BF),
+            vmem((2, LINES, 128), BF),
+            vmem((RD, CD, HC), BF),
+            vmem((RD, CD, HC), F32),
+            vmem((RD, CD, HC), F32),
             vmem((KIN, GATES), F32),
             vmem((1, GATES), F32),
-            pltpu.SemaphoreType.DMA((1 + KS,)),
+            pltpu.SemaphoreType.DMA((PARTS + 3,)),
             pltpu.SemaphoreType.DMA((TAPS + 4,)),
         ],
         compiler_params=pltpu.CompilerParams(vmem_limit_bytes=63 * 1024 * 1024),
@@ -768,7 +764,24 @@
 
 
 def finish(
-    scale, hid, gh, gc, total_hbm, hid_out, gh_out, gc_out, kg_out, bg_out, total, kg, bg, in_sem, sem
+    scale,
+    hid_in,
+    gh_in,
+    gc_in,
+    total_in,
+    hid_out,
+    gh_out,
+    gc_out,
+    kg_out,
+    bg_out,
+    total,
+    hid,
+    gh,
+    gc,
+    kg,
+    bg,
+    in_sem,
+    sem,
 ):
     copies = []
 
@@ -778,27 +791,41 @@
         copies.append(copy)
 
     fetched = []
-    step = KS * HC
-    for i in range(1 + KS):
-        at = pl.ds(TAPS * HC if i == 0 else (i - 1) * step, step)
-        copy = pltpu.make_async_copy(total_hbm.at[at, :], total.at[at, :], in_sem.at[i])
+
+    def fetch(src, dst):
+        copy = pltpu.make_async_copy(src, dst, in_sem.at[len(fetched)])
         copy.start()
         fetched.append(copy)
-    put(hid, hid_out)
-    put(gh, gh_out)
-    put(gc, gc_out)
-    fetched[0].wait()
-    for tap in range(TAPS):
-        a, b = divmod(tap, KS)
-        if b == 0:
-            fetched[1 + a].wait()
-        first = TAPS * HC + a * 128 + b * CI
-        at = tap * 160
-        kg[pl.ds(at, CI), :] = total[pl.ds(first, CI), :].astype(F32) * scale
-        kg[pl.ds(at + CI, HC), :] = total[pl.ds(tap * HC, HC), :].astype(F32) * scale
-        put(kg.at[pl.ds(at, 160), :], kg_out.at[pl.ds(at, 160), :])
-    bg[...] = total[pl.ds(BIAS_ROW, 16), :].astype(F32)[:1, :] * scale
+
+    for base, lines in AREAS[::-1]:
+        area = pl.ds(base, 2 * lines)
+        fetch(total_in.at[:, area, :], total.at[:, area, :])
+    for src, dst in ((hid_in, hid), (gh_in, gh), (gc_in, gc)):
+        fetch(src, dst)
+
+    def take(core, panel, p, row, count):
+        base, lines = AREAS[p]
+        return total[core, pl.ds(base + panel * lines + row, count), :].astype(F32) * scale
+
+    for p in (2, 1, 0):
+        fetched[2 - p].wait()
+        for b in range(KS):
+            at = (p * KS + b) * 160
+            for core in range(2):
+                for panel in range(2):
+                    cols = pl.ds((2 * core + panel) * 128, 128)
+                    kg[pl.ds(at, CI), cols] = take(
+                        core, panel, 2, KS * HC + FRAME_ROWS[p][0] + b * CI, CI
+                    )
+                    kg[pl.ds(at + CI, HC), cols] = take(core, panel, p, b * HC, HC)
+            put(kg.at[pl.ds(at, 160), :], kg_out.at[pl.ds(at, 160), :])
+    for core in range(2):
+        for panel in range(2):
+            bg[:, pl.ds((2 * core + panel) * 128, 128)] = take(core, panel, 2, BIAS_ROW, 16)[:1, :]
     put(bg, bg_out)
+    for i, (src, dst) in enumerate(((hid, hid_out), (gh, gh_out), (gc, gc_out))):
+        fetched[PARTS + i].wait()
+        put(src, dst)
     for copy in copies:
         copy.wait()
 

time: 70.5 us -> 68 us (0.965)
  Pallas kernels: 69.7 us -> 67.2 us
    pallas_call x1, Pallas kernels: 6.24 us -> 2.95 us  [shards(): pl.pallas_call(functools.partial(finish, scale), out_shape=(jax.ShapeDtyp...]
    pallas_call x1, Pallas kernels: 63.5 us -> 64.3 us  [shards(): pl.pallas_call(functools.partial(body, n_rows, n_cols), out_shape=(jax.Sh...]
where the time goes in v4:
time: 68 us; the launch traced here: 67.9 us
  Pallas kernels  67.2 us (99%)
    pallas_call x1, Pallas kernels, shards(): pl.pallas_call(functools.partial(body, n_rows, n_cols), out_shape=(jax.Sh...  64.3 us
    pallas_call x1, Pallas kernels, shards(): pl.pallas_call(functools.partial(finish, scale), out_shape=(jax.ShapeDtyp...  2.95 us

profile of v4, /device:TPU:1, one launch (start us, length us, event | category | flops | bytes accessed | tf_op | source)
XLA Modules:
  0.0 67.9 jit_solution(800252003325183897)
XLA Ops:
  0.6 64.3 %shard_map.101 = (bf16[4,32,128]{2,1,0:T(8,128)(2,1)}, f32[4,32,128]{2,1,0:T(8,128)}, f32[4,32,128]{2,1,0:T(8,128)}, bf16[2,2944,128]{2,1,0:T(8,128)(2,1)}) custom-call(bf16[2,4,1024]{2,1,0:T(4,128)(2,1)} %frames_ref.1, bf16[4,32,128]{2,1,0:T(8,128)(2,1)} %hidden_ref.1, f32[4,32,128]{2,1,0:T(8,128)} %cell_ref.1, bf16[1440,512]{1,0:T(8,128)(2,1)} %kernel_ref.1, ...), custom_call_target="tpu_custom_call" | custom-call | tf_op jit(solution)/shard_map/pallas_call | solution.py:724
  64.9 3.0 %shard_map.102 = (bf16[4,32,128]{2,1,0:T(8,128)(2,1)}, f32[4,32,128]{2,1,0:T(8,128)}, f32[4,32,128]{2,1,0:T(8,128)}, f32[1440,512]{1,0:T(8,128)}, f32[1,512]{1,0:T(1,128)}) custom-call(bf16[4,32,128]{2,1,0:T(8,128)(2,1)} %get-tuple-element.14.hid_in, f32[4,32,128]{2,1,0:T(8,128)} %get-tuple-element.15.gh_in, f32[4,32,128]{2,1,0:T(8,128)} %get-tuple-element.16.gc_in, ...), custom_call_target="tpu_custom_call" | custom-call | tf_op jit(solution)/shard_map/pallas_call | solution.py:740

commit v5 on v4

--- a/solution.py
+++ b/solution.py
@@ -34,6 +34,7 @@
 FRAME_ROWS = ((0, 112), (112, 96), (208, 96))
 AREAS = ((0, 384), (768, 384), (1536, 704))
 LINES = 2944
+ORDER = (2, 0, 1)
 BIAS_ROW = 384 + 3 * CI
 SIDES = [(dr, dc) for dr in (-1, 0, 1) for dc in (-1, 0, 1) if (dr, dc) != (0, 0)]
 
@@ -44,6 +45,10 @@
     if step > 0:
         return (size - halo, halo), (0, halo)
     return (0, halo), (halo + size, halo)
+
+
+def far_first(n):
+    return sorted(range(1, n), key=lambda d: (-min(d, n - d), d))
 
 
 def place(x, y, z, core):
@@ -481,14 +486,15 @@
                     out[pl.ds(at + KS * HC + first, size_a), :] = cut[start : start + size_a, :]
                 out[pl.ds(at + lines - 16, 16), :] = jnp.zeros((16, 128), out.dtype)
 
-    swaps = []
-    for p, (base, lines) in enumerate(AREAS):
+    swaps = [None] * PARTS
+    for p in ORDER:
+        base, lines = AREAS[p]
         weight_grad(p, other_at, a0)
         area = pl.ds(base, 2 * lines)
         copy = copy_to(a0.at[area, :], r0.at[area, :], sibling)
         copy.start()
-        swaps.append(copy)
-    for p in range(PARTS):
+        swaps[p] = copy
+    for p in ORDER:
         weight_grad(p, mine_at, o0)
     sent += swaps
 
@@ -498,28 +504,30 @@
         ("x", "z", "y", r1x, a2x, r2x, r3x, g4x),
     ]
 
-    stage1 = []
-    for p, (ax1, ax2, ax3, r1, a2, r2, r3, g4) in enumerate(plans):
+    stage1 = [None] * PARTS
+    for p in ORDER:
+        ax1, ax2, ax3, r1, a2, r2, r3, g4 = plans[p]
         base, lines = AREAS[p]
         n1, chunk = size[ax1], r1.shape[1]
         swaps[p].wait_recv()
         area = pl.ds(base, 2 * lines)
         a1[area, :] = (o0[area, :] + r0[area, :].astype(F32)).astype(BF)
         copies = []
-        for d in range(1, n1):
+        for d in far_first(n1):
             to = pl.multiple_of(base + lax.rem(mine[ax1] + d, n1) * chunk, 16)
             copy = copy_to(a1.at[pl.ds(to, chunk), :], r1.at[d - 1], peer(ax1, d))
             copy.start()
             copies.append(copy)
-        stage1.append(copies)
+        stage1[p] = copies
         sent += copies
 
     adjoint(dgo, RD)
     zs[pl.ds(EDGE + RD * WD, EDGE), :] = wide
     for k in range(RD + 2):
         cb[k] = gathered(k - 2, RD)
-    stage2 = []
-    for p, (ax1, ax2, ax3, r1, a2, r2, r3, g4) in enumerate(plans):
+    stage2 = [None] * PARTS
+    for p in ORDER:
+        ax1, ax2, ax3, r1, a2, r2, r3, g4 = plans[p]
         base, lines = AREAS[p]
         n1, chunk = size[ax1], r1.shape[1]
         n2, unit = size[ax2], r2.shape[1]
@@ -531,12 +539,12 @@
             total = total + r1[d - 1].astype(F32)
         a2[pl.ds(0, chunk), :] = total.astype(BF)
         copies = []
-        for d in range(1, n2):
+        for d in far_first(n2):
             to = pl.multiple_of(lax.rem(mine[ax2] + d, n2) * unit, 16)
             copy = copy_to(a2.at[pl.ds(to, unit), :], r2.at[d - 1], peer(ax2, d))
             copy.start()
             copies.append(copy)
-        stage2.append(copies)
+        stage2[p] = copies
         sent += copies
 
     late = []
@@ -555,8 +563,9 @@
         late.append(copy)
     sent += late
 
-    stage3 = []
-    for p, (ax1, ax2, ax3, r1, a2, r2, r3, g4) in enumerate(plans):
+    stage3 = [None] * PARTS
+    for p in ORDER:
+        ax1, ax2, ax3, r1, a2, r2, r3, g4 = plans[p]
         n2, n3, unit = size[ax2], size[ax3], r2.shape[1]
         for copy in stage2[p]:
             copy.wait_recv()
@@ -565,15 +574,16 @@
             total = total + r2[d - 1].astype(F32)
         r3[mine[ax3]] = total.astype(BF)
         copies = []
-        for d in range(1, n3):
+        for d in far_first(n3):
             copy = copy_to(r3.at[mine[ax3]], r3.at[mine[ax3]], peer(ax3, d))
             copy.start()
             copies.append(copy)
-        stage3.append(copies)
+        stage3[p] = copies
         sent += copies
 
-    stage4 = []
-    for p, (ax1, ax2, ax3, r1, a2, r2, r3, g4) in enumerate(plans):
+    stage4 = [None] * PARTS
+    for p in ORDER:
+        ax1, ax2, ax3, r1, a2, r2, r3, g4 = plans[p]
         n2, n3, unit = size[ax2], size[ax3], r2.shape[1]
         for copy in stage3[p]:
             copy.wait_recv()
@@ -583,27 +593,28 @@
         slot = g4.at[pl.ds(pl.multiple_of(mine[ax2] * unit, 16), unit), :]
         slot[...] = total.astype(BF)
         copies = []
-        for d in range(1, n2):
+        for d in far_first(n2):
             copy = copy_to(slot, slot, peer(ax2, d))
             copy.start()
             copies.append(copy)
-        stage4.append(copies)
+        stage4[p] = copies
         sent += copies
 
-    stage5 = []
-    for p, (ax1, ax2, ax3, r1, a2, r2, r3, g4) in enumerate(plans):
+    stage5 = [None] * PARTS
+    for p in ORDER:
+        ax1, ax2, ax3, r1, a2, r2, r3, g4 = plans[p]
         base, lines = AREAS[p]
         n1, chunk = size[ax1], r1.shape[1]
         for copy in stage4[p]:
             copy.wait_recv()
         at = pl.ds(pl.multiple_of(base + mine[ax1] * chunk, 16), chunk)
         copies = []
-        for d in range(1, n1):
+        for d in far_first(n1):
             copy = copy_to(g4.at[pl.ds(0, chunk), :], gs.at[core, at, :], peer(ax1, d))
             copy.start()
             copies.append(copy)
         gs[core, at, :] = g4[pl.ds(0, chunk), :]
-        stage5.append(copies)
+        stage5[p] = copies
         sent += copies
 
     for copy in late:
@@ -620,18 +631,20 @@
 
     write(gh_out, gh_hbm)
 
-    stage6 = []
-    for p, (base, lines) in enumerate(AREAS):
+    stage6 = [None] * PARTS
+    for p in ORDER:
+        base, lines = AREAS[p]
         for copy in stage5[p]:
             copy.wait_recv()
         slot = gs.at[core, pl.ds(base, 2 * lines), :]
         copy = copy_to(slot, slot, sibling)
         copy.start()
-        stage6.append(copy)
+        stage6[p] = copy
         write(slot, total_hbm.at[core, pl.ds(base, 2 * lines), :])
     sent += stage6
-    for p, copy in enumerate(stage6):
+    for p in ORDER:
         base, lines = AREAS[p]
+        copy = stage6[p]
         copy.wait_recv()
         area = pl.ds(base, 2 * lines)
         write(gs.at[1 - core, area, :], total_hbm.at[1 - core, area, :])

time: 68 us -> 63 us (0.926)
  Pallas kernels: 67.2 us -> 62.2 us
    pallas_call x1, Pallas kernels: 64.3 us -> 59.3 us  [shards(): pl.pallas_call(functools.partial(body, n_rows, n_cols), out_shape=(jax.Sh...]
where the time goes in v5:
time: 63 us; the launch traced here: 62.9 us
  Pallas kernels  62.2 us (99%)
  between operations  0.64 us (1%)
    pallas_call x1, Pallas kernels, shards(): pl.pallas_call(functools.partial(body, n_rows, n_cols), out_shape=(jax.Sh...  59.3 us
    pallas_call x1, Pallas kernels, shards(): pl.pallas_call(functools.partial(finish, scale), out_shape=(jax.ShapeDtyp...  2.95 us

profile of v5, /device:TPU:1, one launch (start us, length us, event | category | flops | bytes accessed | tf_op | source)
XLA Modules:
  0.0 62.9 jit_solution(851674754655222184)
XLA Ops:
  0.6 59.3 %shard_map.101 = (bf16[4,32,128]{2,1,0:T(8,128)(2,1)}, f32[4,32,128]{2,1,0:T(8,128)}, f32[4,32,128]{2,1,0:T(8,128)}, bf16[2,2944,128]{2,1,0:T(8,128)(2,1)}) custom-call(bf16[2,4,1024]{2,1,0:T(4,128)(2,1)} %frames_ref.1, bf16[4,32,128]{2,1,0:T(8,128)(2,1)} %hidden_ref.1, f32[4,32,128]{2,1,0:T(8,128)} %cell_ref.1, bf16[1440,512]{1,0:T(8,128)(2,1)} %kernel_ref.1, ...), custom_call_target="tpu_custom_call" | custom-call | tf_op jit(solution)/shard_map/pallas_call | solution.py:737
  59.9 3.0 %shard_map.102 = (bf16[4,32,128]{2,1,0:T(8,128)(2,1)}, f32[4,32,128]{2,1,0:T(8,128)}, f32[4,32,128]{2,1,0:T(8,128)}, f32[1440,512]{1,0:T(8,128)}, f32[1,512]{1,0:T(1,128)}) custom-call(bf16[4,32,128]{2,1,0:T(8,128)(2,1)} %get-tuple-element.14.hid_in, f32[4,32,128]{2,1,0:T(8,128)} %get-tuple-element.15.gh_in, f32[4,32,128]{2,1,0:T(8,128)} %get-tuple-element.16.gc_in, ...), custom_call_target="tpu_custom_call" | custom-call | tf_op jit(solution)/shard_map/pallas_call | solution.py:753

commit v6 on v5

--- a/solution.py
+++ b/solution.py
@@ -510,14 +510,15 @@
         base, lines = AREAS[p]
         n1, chunk = size[ax1], r1.shape[1]
         swaps[p].wait_recv()
-        area = pl.ds(base, 2 * lines)
-        a1[area, :] = (o0[area, :] + r0[area, :].astype(F32)).astype(BF)
         copies = []
-        for d in far_first(n1):
+        for d in far_first(n1) + [0]:
             to = pl.multiple_of(base + lax.rem(mine[ax1] + d, n1) * chunk, 16)
-            copy = copy_to(a1.at[pl.ds(to, chunk), :], r1.at[d - 1], peer(ax1, d))
-            copy.start()
-            copies.append(copy)
+            at = pl.ds(to, chunk)
+            a1[at, :] = (o0[at, :] + r0[at, :].astype(F32)).astype(BF)
+            if d > 0:
+                copy = copy_to(a1.at[at, :], r1.at[d - 1], peer(ax1, d))
+                copy.start()
+                copies.append(copy)
         stage1[p] = copies
         sent += copies
 
@@ -641,7 +642,8 @@
         copy.start()
         stage6[p] = copy
         write(slot, total_hbm.at[core, pl.ds(base, 2 * lines), :])
-    sent += stage6
+    for copy in halos + sent:
+        copy.wait_send()
     for p in ORDER:
         base, lines = AREAS[p]
         copy = stage6[p]
@@ -649,12 +651,10 @@
         area = pl.ds(base, 2 * lines)
         write(gs.at[1 - core, area, :], total_hbm.at[1 - core, area, :])
 
+    for copy in stage6:
+        copy.wait_send()
     for copy in written:
         copy.wait()
-    for copy in halos:
-        copy.wait_send()
-    for copy in sent:
-        copy.wait_send()
 
 
 def sizes(p, n1, n2):

time: 63 us -> 62.8 us (level)
  no operation moved by 1% of the time
where the time goes in v6:
time: 62.8 us; the launch traced here: 62.7 us
  Pallas kernels  62 us (99%)
  between operations  0.64 us (1%)
    pallas_call x1, Pallas kernels, shards(): pl.pallas_call(functools.partial(body, n_rows, n_cols), out_shape=(jax.Sh...  59.1 us
    pallas_call x1, Pallas kernels, shards(): pl.pallas_call(functools.partial(finish, scale), out_shape=(jax.ShapeDtyp...  2.95 us

profile of v6, /device:TPU:1, one launch (start us, length us, event | category | flops | bytes accessed | tf_op | source)
XLA Modules:
  0.0 62.7 jit_solution(717806214629472358)
XLA Ops:
  0.6 59.1 %shard_map.101 = (bf16[4,32,128]{2,1,0:T(8,128)(2,1)}, f32[4,32,128]{2,1,0:T(8,128)}, f32[4,32,128]{2,1,0:T(8,128)}, bf16[2,2944,128]{2,1,0:T(8,128)(2,1)}) custom-call(bf16[2,4,1024]{2,1,0:T(4,128)(2,1)} %frames_ref.1, bf16[4,32,128]{2,1,0:T(8,128)(2,1)} %hidden_ref.1, f32[4,32,128]{2,1,0:T(8,128)} %cell_ref.1, bf16[1440,512]{1,0:T(8,128)(2,1)} %kernel_ref.1, ...), custom_call_target="tpu_custom_call" | custom-call | tf_op jit(solution)/shard_map/pallas_call | solution.py:737
  59.7 3.0 %shard_map.102 = (bf16[4,32,128]{2,1,0:T(8,128)(2,1)}, f32[4,32,128]{2,1,0:T(8,128)}, f32[4,32,128]{2,1,0:T(8,128)}, f32[1440,512]{1,0:T(8,128)}, f32[1,512]{1,0:T(1,128)}) custom-call(bf16[4,32,128]{2,1,0:T(8,128)(2,1)} %get-tuple-element.14.hid_in, f32[4,32,128]{2,1,0:T(8,128)} %get-tuple-element.15.gh_in, f32[4,32,128]{2,1,0:T(8,128)} %get-tuple-element.16.gc_in, ...), custom_call_target="tpu_custom_call" | custom-call | tf_op jit(solution)/shard_map/pallas_call | solution.py:753

commit v7 on v6

--- a/solution.py
+++ b/solution.py
@@ -156,7 +156,7 @@
     greet = [neighbour(dr, dc) for dr, dc in SIDES] + [sibling]
     for axis in ("x", "y", "z"):
         greet += [peer(axis, d) for d in range(1, size[axis])]
-    for who in greet:
+    for who in greet[: len(SIDES)]:
         pl.semaphore_signal(barrier, inc=1, device_id=who, device_id_type=MESH)
 
     local = []
@@ -170,14 +170,8 @@
     fetch(cell_ref, cown)
     fetch(cot_ref, kown)
     fetch(frames_ref, fl.at[1, :, :, pl.ds(128, CD * CI)])
-    fetch(bias_ref, bias_in)
-    for tap in range(TAPS):
-        a, b = divmod(tap, KS)
-        fetch(kernel_ref.at[pl.ds(tap * 160 + CI, HC), :], wp.at[pl.ds(tap * HC, HC), :])
-        fetch(
-            kernel_ref.at[pl.ds(tap * 160, CI), :],
-            wp.at[pl.ds(TAPS * HC + a * 128 + b * CI, CI), :],
-        )
+    for who in greet[len(SIDES) :]:
+        pl.semaphore_signal(barrier, inc=1, device_id=who, device_id_type=MESH)
     for copy in local[:3]:
         copy.wait()
     fields = (
@@ -233,6 +227,14 @@
             copy.start()
             halos.append(copy)
 
+    fetch(bias_ref, bias_in)
+    for tap in range(TAPS):
+        a, b = divmod(tap, KS)
+        fetch(kernel_ref.at[pl.ds(tap * 160 + CI, HC), :], wp.at[pl.ds(tap * HC, HC), :])
+        fetch(
+            kernel_ref.at[pl.ds(tap * 160, CI), :],
+            wp.at[pl.ds(TAPS * HC + a * 128 + b * CI, CI), :],
+        )
     for a in range(KS):
         wp[pl.ds(TAPS * HC + a * 128 + 96, 32), :] = jnp.zeros((32, GATES), BF)
     x32[...] = jnp.zeros_like(x32)

time: 62.8 us -> 62.9 us (level)
  no operation moved by 1% of the time
where the time goes in v7:
time: 62.9 us; the launch traced here: 62.7 us
  Pallas kernels  62 us (99%)
  between operations  0.64 us (1%)
    pallas_call x1, Pallas kernels, shards(): pl.pallas_call(functools.partial(body, n_rows, n_cols), out_shape=(jax.Sh...  59.1 us
    pallas_call x1, Pallas kernels, shards(): pl.pallas_call(functools.partial(finish, scale), out_shape=(jax.ShapeDtyp...  2.95 us

profile of v7, /device:TPU:1, one launch (start us, length us, event | category | flops | bytes accessed | tf_op | source)
XLA Modules:
  0.0 62.7 jit_solution(2763249345579824751)
XLA Ops:
  0.6 59.1 %shard_map.101 = (bf16[4,32,128]{2,1,0:T(8,128)(2,1)}, f32[4,32,128]{2,1,0:T(8,128)}, f32[4,32,128]{2,1,0:T(8,128)}, bf16[2,2944,128]{2,1,0:T(8,128)(2,1)}) custom-call(bf16[2,4,1024]{2,1,0:T(4,128)(2,1)} %frames_ref.1, bf16[4,32,128]{2,1,0:T(8,128)(2,1)} %hidden_ref.1, f32[4,32,128]{2,1,0:T(8,128)} %cell_ref.1, bf16[1440,512]{1,0:T(8,128)(2,1)} %kernel_ref.1, ...), custom_call_target="tpu_custom_call" | custom-call | tf_op jit(solution)/shard_map/pallas_call | solution.py:739
  59.7 3.0 %shard_map.102 = (bf16[4,32,128]{2,1,0:T(8,128)(2,1)}, f32[4,32,128]{2,1,0:T(8,128)}, f32[4,32,128]{2,1,0:T(8,128)}, f32[1440,512]{1,0:T(8,128)}, f32[1,512]{1,0:T(1,128)}) custom-call(bf16[4,32,128]{2,1,0:T(8,128)(2,1)} %get-tuple-element.14.hid_in, f32[4,32,128]{2,1,0:T(8,128)} %get-tuple-element.15.gh_in, f32[4,32,128]{2,1,0:T(8,128)} %get-tuple-element.16.gc_in, ...), custom_call_target="tpu_custom_call" | custom-call | tf_op jit(solution)/shard_map/pallas_call | solution.py:755
